TPU v7x, 32 devices: a whole 2x2x4 slice. The times are simulated.
32 devices in a mesh: batch: 8 (over z, y), heads: 4 (over x, core).
Axes of the slice: x: 2, y: 2, z: 4, core: 2. Of those that a mesh axis runs over, the one named last changes fastest.
Arguments:
- tokens_in: bfloat16 [16384, 768], P(('batch', 'heads')), may hold values from -6 to 6
- cotangent: bfloat16 [16384, 768], P(('batch', 'heads')), may hold values from -6 to 6
- half_length: int32 [16], P('batch'), may hold values from 512 to 1024, as said below
- block_perm: int32 [12, 2], replicated, may hold values from 0 to 1, each once within a row
- w_query: bfloat16 [768, 768], P('heads'), may hold values from -0.21875 to 0.21875
- b_query: bfloat16 [768], P('heads'), may hold values from -1.5 to 1.5
- w_key: bfloat16 [768, 768], P('heads'), may hold values from -0.21875 to 0.21875
- w_value: bfloat16 [768, 768], P('heads'), may hold values from -0.21875 to 0.21875
- b_value: bfloat16 [768], P('heads'), may hold values from -1.5 to 1.5
- w_output: bfloat16 [768, 768], P('heads'), may hold values from -0.875 to 0.875
- b_output: bfloat16 [768], replicated, may hold values from -1.5 to 1.5
- norm1_gain: bfloat16 [768], replicated, may hold values from 0.5 to 1.5
- norm1_shift: bfloat16 [768], replicated, may hold values from -1.5 to 1.5
- w_inner: bfloat16 [768, 3072], P(None, 'heads'), may hold values from -0.21875 to 0.21875
- b_inner: bfloat16 [3072], P('heads'), may hold values from -1.5 to 1.5
- w_outer: bfloat16 [3072, 768], P('heads'), may hold values from -0.109375 to 0.109375
- b_outer: bfloat16 [768], replicated, may hold values from -1.5 to 1.5
- norm2_gain: bfloat16 [768], replicated, may hold values from 0.5 to 1.5
- norm2_shift: bfloat16 [768], replicated, may hold values from -1.5 to 1.5
Outputs:
- block_out: bfloat16 [16384, 768], P(('batch', 'heads'))
- grad_tokens: float32 [16384, 768], P(('batch', 'heads'))
- grad_w_query: float32 [768, 768], P('heads')
- grad_b_query: float32 [768], P('heads')
- grad_w_key: float32 [768, 768], P('heads')
- grad_w_value: float32 [768, 768], P('heads')
- grad_b_value: float32 [768], P('heads')
- grad_w_output: float32 [768, 768], P('heads')
- grad_b_output: float32 [768], replicated
- grad_norm1_gain: float32 [768], replicated
- grad_norm1_shift: float32 [768], replicated
- grad_w_inner: float32 [768, 3072], P(None, 'heads')
- grad_b_inner: float32 [3072], P('heads')
- grad_w_outer: float32 [3072, 768], P('heads')
- grad_b_outer: float32 [768], replicated
- grad_norm2_gain: float32 [768], replicated
- grad_norm2_shift: float32 [768], replicated
Inputs may be any that keep to these rules, and one draw needn't show every extreme that they name: `half_length`: each entry is 1024 (one sequence) or 1024 // 2 (two sequences of that length). `block_perm`: each row is a permutation of 0 and 1.
All inputs are finite; a program needn't handle non-finite values.
Results may differ from a plain program's by a relative error of at most 0.015.
Values may be sent and summed in bfloat16 or wider, within the bound.
No kernel may reach another device: no remote copies, remote signals or barrier semaphores. Data moves between devices by JAX's collectives and lax.ppermute only.
A program may use at most 128 MiB of HBM per device.

v0:
```python
import jax
import jax.numpy as jnp
from jax import lax
from jax.sharding import PartitionSpec as P

HEAD_DIM = 64
HALF = 1024


epsilon = 1e-06
masked_score = -1e30


def as_sent(shard):

    def short(part):
        return part.astype(jnp.bfloat16) if part.dtype == jnp.float32 else part

    return jax.tree.map(short, shard)


def contract_rows(left, right):
    return lax.dot_general(
        left, right, (((0,), (0,)), ((), ())), preferred_element_type=jnp.float32
    )


def contract_cols(left, right):
    return lax.dot_general(
        left, right, (((1,), (1,)), ((), ())), preferred_element_type=jnp.float32
    )


def matmul(left, right):
    return jnp.dot(left, right, preferred_element_type=jnp.float32)


def norm_rows(hidden, gain, shift):
    center = jnp.mean(hidden, axis=1, keepdims=True)
    rinv = lax.rsqrt(jnp.mean(hidden * hidden, axis=1, keepdims=True) - center * center + epsilon)
    zhat = (hidden - center) * rinv
    return (zhat * gain.astype(jnp.float32) + shift.astype(jnp.float32), zhat, rinv)


def norm_back(grad_zhat, zhat, rinv):
    first_mean = jnp.mean(grad_zhat, axis=1, keepdims=True)
    second_mean = jnp.mean(grad_zhat * zhat, axis=1, keepdims=True)
    return rinv * (grad_zhat - first_mean - zhat * second_mean)


def block_masks(is_long, swap_flags, quarter):
    within = jnp.arange(quarter) // (quarter // 2)
    allowed = (is_long == 1) | (
        within[None, :, None] ^ swap_flags[:, None, None] == within[None, None, :]
    )
    flipped = (is_long * swap_flags == 1)[None, :, None]
    return (allowed, flipped)


def block_scores(query_blk, key_sel, allowed):
    scores = jnp.einsum(
        "qhd,khd->hqk", query_blk, key_sel, preferred_element_type=jnp.float32
    ) * HEAD_DIM ** (-0.5)
    return jnp.where(allowed, scores, masked_score)


def attend_half(queries, key_rows, value_rows, is_long, swap_flags):
    quarter = queries.shape[0] // 2
    head_count = swap_flags.shape[0]
    query_q = queries.reshape(2, quarter, head_count, HEAD_DIM)
    key_q = key_rows.reshape(2, quarter, head_count, HEAD_DIM)
    value_q = value_rows.reshape(2, quarter, head_count, HEAD_DIM)
    allowed, flipped = block_masks(is_long, swap_flags, quarter)
    mix_parts = []
    lse_parts = []
    for half_side in range(2):
        key_sel = jnp.where(flipped, key_q[1 - half_side], key_q[half_side])
        value_sel = jnp.where(flipped, value_q[1 - half_side], value_q[half_side])
        scores = block_scores(query_q[half_side], key_sel, allowed)
        row_max = jnp.max(scores, axis=-1, keepdims=True)
        exponent = jnp.exp(scores - row_max)
        row_total = jnp.sum(exponent, axis=-1, keepdims=True)
        weights_bf = (exponent / row_total).astype(jnp.bfloat16)
        mixture = jnp.einsum(
            "hqk,khd->qhd", weights_bf, value_sel, preferred_element_type=jnp.float32
        )
        mix_parts.append(mixture.reshape(quarter, -1))
        lse_parts.append(row_max + jnp.log(row_total))
    return (jnp.concatenate(mix_parts, axis=0).astype(jnp.bfloat16), jnp.stack(lse_parts))


def attend_back(queries, key_rows, value_rows, grad_mix, row_lse, is_long, swap_flags):
    quarter = queries.shape[0] // 2
    head_count = swap_flags.shape[0]
    scale = HEAD_DIM ** (-0.5)
    query_q = queries.reshape(2, quarter, head_count, HEAD_DIM)
    key_q = key_rows.reshape(2, quarter, head_count, HEAD_DIM)
    value_q = value_rows.reshape(2, quarter, head_count, HEAD_DIM)
    grad_q = grad_mix.reshape(2, quarter, head_count, HEAD_DIM)
    allowed, flipped = block_masks(is_long, swap_flags, quarter)
    query_parts = []
    key_parts = []
    value_parts = []
    for half_side in range(2):
        key_sel = jnp.where(flipped, key_q[1 - half_side], key_q[half_side])
        value_sel = jnp.where(flipped, value_q[1 - half_side], value_q[half_side])
        scores = block_scores(query_q[half_side], key_sel, allowed)
        weights = jnp.exp(scores - row_lse[half_side])
        grad_weights = jnp.einsum(
            "qhd,khd->hqk", grad_q[half_side], value_sel, preferred_element_type=jnp.float32
        )
        value_parts.append(
            jnp.einsum(
                "hqk,qhd->khd",
                weights.astype(jnp.bfloat16),
                grad_q[half_side],
                preferred_element_type=jnp.float32,
            )
        )
        grad_scores = (
            weights * (grad_weights - jnp.sum(weights * grad_weights, axis=-1, keepdims=True))
        ).astype(jnp.bfloat16)
        query_parts.append(
            jnp.einsum("hqk,khd->qhd", grad_scores, key_sel, preferred_element_type=jnp.float32)
            * scale
        )
        key_parts.append(
            jnp.einsum(
                "hqk,qhd->khd", grad_scores, query_q[half_side], preferred_element_type=jnp.float32
            )
            * scale
        )
    grad_queries = jnp.stack(query_parts)
    grad_keys = jnp.stack(
        [
            jnp.where(flipped, key_parts[1], key_parts[0]),
            jnp.where(flipped, key_parts[0], key_parts[1]),
        ]
    )
    grad_values = jnp.stack(
        [
            jnp.where(flipped, value_parts[1], value_parts[0]),
            jnp.where(flipped, value_parts[0], value_parts[1]),
        ]
    )
    rows = queries.shape[0]
    return (
        grad_queries.reshape(rows, -1).astype(jnp.bfloat16),
        grad_keys.reshape(rows, -1).astype(jnp.bfloat16),
        grad_values.reshape(rows, -1).astype(jnp.bfloat16),
    )


def body(
    tokens_in,
    cotangent,
    half_length,
    block_perm,
    w_query,
    b_query,
    w_key,
    w_value,
    b_value,
    w_output,
    b_output,
    norm1_gain,
    norm1_shift,
    w_inner,
    b_inner,
    w_outer,
    b_outer,
    norm2_gain,
    norm2_shift,
):
    head_count = w_query.shape[0] // HEAD_DIM
    local_width = w_query.shape[0]
    swap_flags = lax.dynamic_slice_in_dim(
        block_perm[:, 0], lax.axis_index("heads") * head_count, head_count
    )
    is_long = (half_length == HALF).astype(jnp.int32)
    full_tokens = lax.all_gather(tokens_in, "heads", axis=0, tiled=True)
    rows = full_tokens.shape[0]
    spans = rows // HALF
    queries = (contract_cols(full_tokens, w_query) + b_query.astype(jnp.float32)).astype(
        jnp.bfloat16
    )
    key_rows = contract_cols(full_tokens, w_key).astype(jnp.bfloat16)
    value_rows = (contract_cols(full_tokens, w_value) + b_value.astype(jnp.float32)).astype(
        jnp.bfloat16
    )

    def forward_span(pieces):
        return attend_half(pieces[0], pieces[1], pieces[2], pieces[3], swap_flags)

    span_mix, span_lse = lax.map(
        forward_span,
        (
            queries.reshape(spans, HALF, local_width),
            key_rows.reshape(spans, HALF, local_width),
            value_rows.reshape(spans, HALF, local_width),
            is_long,
        ),
    )
    attended = span_mix.reshape(rows, local_width)
    own_heads = lax.all_to_all(
        as_sent(attended), "heads", split_axis=0, concat_axis=1, tiled=True
    ).astype(attended.dtype)
    output_weight_all = lax.all_gather(w_output, "heads", axis=0, tiled=True)
    projected = matmul(own_heads, output_weight_all)
    hidden_one = tokens_in.astype(jnp.float32) + projected + b_output.astype(jnp.float32)
    normed, zhat_one, rinv_one = norm_rows(hidden_one, norm1_gain, norm1_shift)
    full_normed = lax.all_gather(normed.astype(jnp.bfloat16), "heads", axis=0, tiled=True)
    inner = matmul(full_normed, w_inner) + b_inner.astype(jnp.float32)
    active = jax.nn.gelu(inner, approximate=False).astype(jnp.bfloat16)
    ffn_sum = lax.psum_scatter(matmul(active, w_outer), "heads", scatter_dimension=0, tiled=True)
    hidden_two = normed + ffn_sum + b_outer.astype(jnp.float32)
    result, zhat_two, rinv_two = norm_rows(hidden_two, norm2_gain, norm2_shift)
    block_out = result.astype(jnp.bfloat16)
    grad_out = cotangent.astype(jnp.float32)
    grad_gain2 = jnp.sum(grad_out * zhat_two, axis=0)
    grad_shift2 = jnp.sum(grad_out, axis=0)
    grad_two = norm_back(grad_out * norm2_gain.astype(jnp.float32), zhat_two, rinv_two)
    grad_b_outer = jnp.sum(grad_two, axis=0)
    full_grad_two = lax.all_gather(grad_two.astype(jnp.bfloat16), "heads", axis=0, tiled=True)
    grad_w_outer = contract_rows(active, full_grad_two)
    grad_active = contract_cols(full_grad_two, w_outer)
    gelu_value, gelu_pull = jax.vjp(lambda values: jax.nn.gelu(values, approximate=False), inner)
    grad_inner = gelu_pull(grad_active)[0].astype(jnp.bfloat16)
    grad_b_inner = jnp.sum(grad_inner, axis=0, dtype=jnp.float32)
    grad_w_inner = contract_rows(full_normed, grad_inner)
    grad_normed = (
        lax.psum_scatter(
            contract_cols(grad_inner, w_inner), "heads", scatter_dimension=0, tiled=True
        )
        + grad_two
    )
    grad_gain1 = jnp.sum(grad_normed * zhat_one, axis=0)
    grad_shift1 = jnp.sum(grad_normed, axis=0)
    grad_one = norm_back(grad_normed * norm1_gain.astype(jnp.float32), zhat_one, rinv_one)
    grad_b_output = jnp.sum(grad_one, axis=0)
    row_sums = lax.psum(
        (grad_b_output, grad_gain1, grad_shift1, grad_b_outer, grad_gain2, grad_shift2),
        ("batch", "heads"),
    )
    grad_attn_in = grad_one.astype(jnp.bfloat16)
    grad_w_output = lax.psum_scatter(
        contract_rows(
            lax.slice_in_dim(own_heads, 0, local_width * lax.axis_size("heads"), axis=1),
            grad_attn_in,
        ).astype(jnp.bfloat16),
        "heads",
        scatter_dimension=0,
        tiled=True,
    ).astype(jnp.float32)
    own_grad = contract_cols(grad_attn_in, output_weight_all).astype(jnp.bfloat16)
    grad_attended = lax.all_to_all(own_grad, "heads", split_axis=1, concat_axis=0, tiled=True)

    def backward_span(pieces):
        return attend_back(
            pieces[0], pieces[1], pieces[2], pieces[3], pieces[4], pieces[5], swap_flags
        )

    span_dq, span_dk, span_dv = lax.map(
        backward_span,
        (
            queries.reshape(spans, HALF, local_width),
            key_rows.reshape(spans, HALF, local_width),
            value_rows.reshape(spans, HALF, local_width),
            grad_attended.reshape(spans, HALF, local_width),
            span_lse,
            is_long,
        ),
    )
    grad_queries = span_dq.reshape(rows, local_width)
    grad_keys = span_dk.reshape(rows, local_width)
    grad_values = span_dv.reshape(rows, local_width)
    grad_b_query = jnp.sum(grad_queries, axis=0, dtype=jnp.float32)
    grad_b_value = jnp.sum(grad_values, axis=0, dtype=jnp.float32)
    grad_w_query = contract_rows(grad_queries, full_tokens)
    grad_w_key = contract_rows(grad_keys, full_tokens)
    grad_w_value = contract_rows(grad_values, full_tokens)
    input_terms = (
        matmul(grad_queries, w_query) + matmul(grad_keys, w_key) + matmul(grad_values, w_value)
    )
    grad_tokens = (
        lax.psum_scatter(
            input_terms.astype(jnp.bfloat16), "heads", scatter_dimension=0, tiled=True
        ).astype(jnp.float32)
        + grad_one
    )
    summed = lax.psum(
        (
            grad_w_query,
            grad_b_query,
            grad_w_key,
            grad_w_value,
            grad_b_value,
            grad_w_output,
            grad_w_inner,
            grad_b_inner,
            grad_w_outer,
        ),
        "batch",
    )
    return (
        block_out,
        grad_tokens,
        summed[0],
        summed[1],
        summed[2],
        summed[3],
        summed[4],
        summed[5],
        row_sums[0],
        row_sums[1],
        row_sums[2],
        summed[6],
        summed[7],
        summed[8],
        row_sums[3],
        row_sums[4],
        row_sums[5],
    )


def solution(mesh):
    placed = (
        P(("batch", "heads"), None),
        P(("batch", "heads"), None),
        P("batch"),
        P(),
        P("heads", None),
        P("heads"),
        P("heads", None),
        P("heads", None),
        P("heads"),
        P("heads", None),
        P(),
        P(),
        P(),
        P(None, "heads"),
        P("heads"),
        P("heads", None),
        P(),
        P(),
        P(),
    )
    return jax.shard_map(
        body,
        mesh=mesh,
        in_specs=placed,
        out_specs=(
            P(("batch", "heads"), None),
            P(("batch", "heads"), None),
            P("heads", None),
            P("heads"),
            P("heads", None),
            P("heads", None),
            P("heads"),
            P("heads", None),
            P(),
            P(),
            P(),
            P(None, "heads"),
            P("heads"),
            P("heads", None),
            P(),
            P(),
            P(),
        ),
        check_vma=False,
    )
```

profile of v0, /device:TPU:0, one launch (start us, length us, event | category | flops | bytes accessed | tf_op | source)
XLA Modules:
  0.0 723.4 jit_solution(6295289893845183994)
XLA Ops:
  11.4 29.4 %all-gather.5.cloned.1.call-done = bf16[2048,768]{1,0:T(8,128)(2,1)} async-done(((bf16[512,768]{1,0:T(8,128)(2,1)}), bf16[2048,768]{1,0:T(8,128)(2,1)}) %all-gather.5.cloned.1.call-update) | async-done | bytes 3145744 | tf_op jit(solution)/shard_map/all_gather | solution.py:181
  40.9 3.2 fusion.45
  47.7 19.5 %while.30 = (s32[]{:T(128)}, bf16[2,1024,192]{1,2,0:T(8,128)(2,1)}, f32[2,2,3,512,1]{3,2,1,4,0:T(4,128)}, s32[2]{0:T(128)S(1)}, s32[3]{0:T(128)S(1)}, /*index=5*...) while((s32[]{:T(128)}, bf16[2,1024,192]{1,2,0:T(8,128)(2,1)}, ...), condition=%wide.region_5.6_spmd, body=%wide.region_0.5_spmd.sunk | while | flops 419763712 | bytes 27093852 | solution.py:195
  50.5 2.4 fusion.163
  60.3 2.4 fusion.163
  67.7 2.8 copy.115
  70.5 3.3 all_to_all.26
  73.8 2.2 copy.116
  76.0 4.2 all-to-all-start
  81.6 10.3 %all-to-all-done = bf16[4,512,192]{1,2,0:T(8,128)(2,1)} async-done(((bf16[4,512,192]{1,2,0:T(8,128)(2,1)}), bf16[4,512,192]{1,2,0:T(8,128)(2,1)}, u32[]{:S(2)}, u32[]{:S(2)}) %all-to-all-start) | async-done | bytes 786464 | tf_op jit(solution)/shard_map/all_to_all | solution.py:205
  91.9 2.8 fusion.58
  98.9 26.9 %all-gather.9.cloned.1.call-done = bf16[2048,768]{1,0:T(8,128)(2,1)} async-done(((bf16[512,768]{1,0:T(8,128)(2,1)}), bf16[2048,768]{1,0:T(8,128)(2,1)}) %all-gather.9.cloned.1.call-update) | async-done | bytes 3145744 | tf_op jit(solution)/shard_map/all_gather | solution.py:212
  125.8 18.4 %multiply_convert_fusion.2 = (bf16[2048,768]{1,0:T(8,128)(2,1)S(1)}, f32[2048,768]{1,0:T(8,128)}, f32[2048,768]{1,0:T(8,128)}) fusion(f32[768]{0:T(1024)} %convert_element_type.191, bf16[2048,768]{1,0:T(8,128)(2,1)} %all-gather.9.cloned.1.call-done, bf16[768,768]{1,0:T(8,128)(2,1)S(1)} %copy-done), kind=kOutput, calls=%fused_computation.106 | convolution fusion | flops 2519728128 | bytes 20057088 | tf_op jit(solution)/shard_map/dot_general | solution.py:35
  144.2 1.7 copy-done.57
  145.9 4.5 fusion.65
  154.3 54.6 %reduce-scatter.5.cloned.1.call-done = f32[512,768]{1,0:T(8,128)} async-done(((f32[2048,768]{1,0:T(8,128)}), f32[512,768]{1,0:T(8,128)}) %reduce-scatter.5.cloned.1.call-update) | async-done | bytes 1572880 | tf_op jit(solution)/shard_map/reduce_scatter | solution.py:215
  208.9 2.6 fusion.57
  212.9 2.1 fusion.59
  217.4 28.5 %all-gather.11.cloned.1.call-done = bf16[2048,768]{1,0:T(8,128)(2,1)} async-done(((bf16[512,768]{1,0:T(8,128)(2,1)}), bf16[2048,768]{1,0:T(8,128)(2,1)}) %all-gather.11.cloned.1.call-update) | async-done | bytes 3145744 | tf_op jit(solution)/shard_map/all_gather | solution.py:224
  245.9 11.0 %convert_reduce_fusion = (f32[768]{0:T(1024)}, bf16[2048,768]{1,0:T(8,128)(2,1)S(1)}) fusion(f32[2048,768]{1,0:T(8,128)} %get-tuple-element.415, f32[2048,768]{1,0:T(8,128)} %get-tuple-element.458, f32[768]{0:T(1024)} %convert_element_type.191, bf16[2048,768]{1,0:T(8,128)(2,1)} %all-gather.11.cloned.1.call-done, bf16[768,768]{1,0:T(8,128)(2,1)} %param.38), kind=kOutput, calls=%fused_computation.103 | convolution fusion | flops 2442657024 | bytes 20060160 | tf_op jit(solution)/shard_map/dot_general | solution.py:29
  256.9 1.7 copy-done.58
  258.5 4.5 fusion.66
  263.1 58.5 %reduce-scatter.7.cloned.1.call-done = f32[512,768]{1,0:T(8,128)} async-done(((f32[2048,768]{1,0:T(8,128)}), f32[512,768]{1,0:T(8,128)}) %reduce-scatter.7.cloned.1.call-update) | async-done | bytes 1572880 | tf_op jit(solution)/shard_map/reduce_scatter | solution.py:232
  321.6 3.9 multiply_reduce_fusion.2
  329.7 3.5 all-to-all-start.1
  333.3 3.5 convolution_convert_fusion.1
  336.9 8.0 %all-to-all-done.1 = bf16[512,4,192]{0,2,1:T(8,128)(2,1)S(1)} async-done(((bf16[512,4,192]{0,2,1:T(8,128)(2,1)}), bf16[512,4,192]{0,2,1:T(8,128)(2,1)S(1)}, u32[]{:S(2)}, u32[]{:S(2)}) %all-to-all-start.1) | async-done | bytes 786464 | tf_op jit(solution)/shard_map/all_to_all | solution.py:256
  344.9 1.5 copy.118
  346.4 2.5 reshape.454
  352.8 69.4 %while.31 = (s32[]{:T(128)}, bf16[2,1024,192]{1,2,0:T(8,128)(2,1)}, bf16[2,1024,192]{1,2,0:T(8,128)(2,1)}, bf16[2,1024,192]{1,2,0:T(8,128)(2,1)}, s32[2]{0:T(128...) while((s32[]{:T(128)}, bf16[2,1024,192]{1,2,0:T(8,128)(2,1)}, ...), condition=%wide.region_19.20_spmd, body=%wide.region_16.19_spmd.sunk | while | flops 1026296320 | bytes 104685784 | solution.py:263
  354.4 1.8 constant_dynamic-slice_fusion.20
  357.6 2.9 constant_dynamic-slice_fusion.21
  362.0 2.8 multiply_reduce_fusion.10
  364.9 2.8 multiply_convert_fusion.6
  369.6 1.7 multiply_reduce_fusion.9
  372.7 1.4 fusion.189
  375.3 2.0 convert_element_type.279
  377.3 1.8 constant_dynamic-update-slice_fusion.8
  381.3 2.0 convert_element_type.278
  383.3 1.8 constant_dynamic-update-slice_fusion.7
  388.9 1.8 constant_dynamic-slice_fusion.20
  392.0 2.9 constant_dynamic-slice_fusion.21
  396.4 2.8 multiply_reduce_fusion.10
  399.3 2.8 multiply_convert_fusion.6
  404.0 1.7 multiply_reduce_fusion.9
  409.7 2.0 convert_element_type.279
  411.7 1.8 constant_dynamic-update-slice_fusion.8
  415.7 2.0 convert_element_type.278
  417.7 1.8 constant_dynamic-update-slice_fusion.7
  426.9 2.8 add_convert_fusion
  429.8 7.1 fusion.73
  436.9 4.2 fusion.72
  441.0 1.7 fusion.69
  442.7 1.7 fusion.70
  444.3 1.7 fusion.71
  446.8 40.5 %all-reduce = (f32[768]{0:T(1024)}, f32[768]{0:T(1024)}, f32[768]{0:T(1024)}, f32[768]{0:T(1024)}, f32[768]{0:T(1024)}, /*index=5*/f32[768]{0:T(1024)}) all-reduce(f32[768]{0:T(1024)S(1)} %copy-done.44, f32[768]{0:T(1024)S(1)} %copy-done.47, f32[768]{0:T(1024)S(1)} %copy-done.48, ...), channel_id=1, replica_groups=mesh['batch'=8,'heads'=4] {'batch','heads'}, use_global_device_ids=true, to_apply=%region_31.32 | all-reduce | flops 4608 | bytes 36864 | tf_op jit(solution)/shard_map/psum | solution.py:241
  487.7 58.3 %all-reduce.7 = (f32[192]{0:T(256)}, f32[192]{0:T(256)}, f32[192,768]{1,0:T(8,128)}, f32[768]{0:T(1024)}) all-reduce(f32[192]{0:T(256)S(1)} %convert_reduce_fusion.3, f32[192]{0:T(256)S(1)} %convert_reduce_fusion.2, bf16[192,768]{1,0:T(8,128)(2,1)} %reduce-scatter.11.cloned.1.call-done, ...), channel_id=1, replica_groups=mesh['batch'=8,'heads'=4] {'batch'}, use_global_device_ids=true, to_apply=%region_23.24 | all-reduce | flops 148608 | bytes 893952 | tf_op jit(solution)/shard_map/psum | solution.py:291
  546.0 2.4 convert_add_fusion
  548.4 159.1 %all-reduce.6.cloned.1.call-done = (f32[192,768]{1,0:T(8,128)}, f32[192,768]{1,0:T(8,128)}, f32[192,768]{1,0:T(8,128)}, f32[768,768]{1,0:T(8,128)}, f32[768,768]{1,0:T(8,128)}) async-done(((f32[192,768]{1,0:T(8,128)}, f32[192,768]{1,0:T(8,128)}, f32[192,768]{1,0:T(8,128)}, f32[768,768]{1,0:T(8,128)}, f32[768,768]{1,0:T(8,128)}), (f32[192,768]{1,0:T(8,128)}, f32[192,768]{1,0:T(8,128)}, f32[192,768]{1,0:T(8,128)}, ...) | async-done | bytes 6488080 | tf_op jit(solution)/shard_map/psum | solution.py:291
  707.5 2.1 copy.187
  709.6 1.9 copy.188
  711.5 2.1 copy.189
  713.6 1.4 copy.190
  715.0 1.4 copy.191
  (295 shorter events, 75.4 us)
Async XLA Ops:
  7.2 118.6 %copy-start = (bf16[768,768]{1,0:T(8,128)(2,1)S(1)}, bf16[768,768]{1,0:T(8,128)(2,1)}, u32[]{:S(2)}) copy-start(bf16[768,768]{1,0:T(8,128)(2,1)} %param.36) | copy-start | bytes 3538948
  7.2 33.7 %all-gather.5.cloned.1.call-start = ((), (), s32[]{:S(2)}) async-start(), calls=%async_computation.6 | async-start | bytes 3932160 | tf_op jit(solution)/shard_map/all_gather | solution.py:181
  7.9 73.6 %all-gather.7.cloned.1.call-start = ((), (), s32[]{:S(2)}) async-start(), calls=%async_computation.7 | async-start | bytes 1474560 | tf_op jit(solution)/shard_map/all_gather | solution.py:208
  11.4 32.7 %copy-start.35 = (bf16[192,768]{1,0:T(8,128)(2,1)S(1)}, bf16[192,768]{1,0:T(8,128)(2,1)}, u32[]{:S(2)}) copy-start(bf16[192,768]{1,0:T(8,128)(2,1)} %param.29) | copy-start | bytes 884740
  40.9 3.3 copy-start.10
  50.5 2.9 copy-start.27
  50.5 2.9 copy-start.28
  50.5 2.9 copy-start.29
  53.4 1.7 copy-start.38
  60.3 2.9 copy-start.27
  60.3 2.9 copy-start.28
  60.3 2.9 copy-start.29
  63.2 1.7 copy-start.38
  67.6 12.6 %copy-start.50 = (bf16[768]{0:T(1024)(128)(2,1)S(1)}, bf16[768]{0:T(1024)(128)(2,1)}, u32[]{:S(2)}) copy-start(bf16[768]{0:T(1024)(128)(2,1)} %param.33) | copy-start | bytes 4612
  67.7 12.6 %copy-start.51 = (bf16[768]{0:T(1024)(128)(2,1)S(1)}, bf16[768]{0:T(1024)(128)(2,1)}, u32[]{:S(2)}) copy-start(bf16[768]{0:T(1024)(128)(2,1)} %param.34) | copy-start | bytes 4612
  76.0 15.9 %all-to-all-start = ((bf16[4,512,192]{1,2,0:T(8,128)(2,1)}), bf16[4,512,192]{1,2,0:T(8,128)(2,1)}, u32[]{:S(2)}, u32[]{:S(2)}) async-start(bf16[4,512,192]{1,2,0:T(8,128)(2,1)} %copy.116), calls=%async_computation | async-start | bytes 1572864 | tf_op jit(solution)/shard_map/all_to_all | solution.py:205
  80.2 45.6 %all-gather.9.cloned.1.call-start = ((), (), s32[]{:S(2)}) async-start(), calls=%async_computation.8 | async-start | bytes 3932160 | tf_op jit(solution)/shard_map/all_gather | solution.py:212
  91.9 4.0 copy-start.40
  97.1 111.8 %reduce-scatter.5.cloned.1.call-start = ((), (), s32[]{:S(2)}) async-start(), calls=%async_computation.9 | async-start | bytes 7864320 | tf_op jit(solution)/shard_map/reduce_scatter | solution.py:215
  125.8 20.1 %copy-start.53 = (bf16[768,768]{1,0:T(8,128)(2,1)S(1)}, bf16[768,768]{1,0:T(8,128)(2,1)}, u32[]{:S(2)}) copy-start(bf16[768,768]{1,0:T(8,128)(2,1)} %param.38) | copy-start | bytes 3538948
  144.2 1.7 copy-start.57
  150.4 95.5 %all-gather.11.cloned.1.call-start = ((), (), s32[]{:S(2)}) async-start(), calls=%async_computation.10 | async-start | bytes 3932160 | tf_op jit(solution)/shard_map/all_gather | solution.py:224
  208.9 2.7 copy-start.30
  208.9 2.7 copy-start.41
  208.9 4.0 copy-start.45
  217.2 104.4 %reduce-scatter.7.cloned.1.call-start = ((), (), s32[]{:S(2)}) async-start(), calls=%async_computation.11 | async-start | bytes 7864320 | tf_op jit(solution)/shard_map/reduce_scatter | solution.py:232
  256.9 1.7 copy-start.58
  321.6 3.9 copy-start.19
  325.5 2.3 copy-start.54
  329.7 15.1 %all-to-all-start.1 = ((bf16[512,4,192]{0,2,1:T(8,128)(2,1)}), bf16[512,4,192]{0,2,1:T(8,128)(2,1)S(1)}, u32[]{:S(2)}, u32[]{:S(2)}) async-start(bf16[512,4,192]{0,2,1:T(8,128)(2,1)} %bitcast.260), calls=%async_computation.3 | async-start | bytes 1572864 | tf_op jit(solution)/shard_map/all_to_all | solution.py:256
  333.3 154.4 %reduce-scatter.11.cloned.1.call-start = ((), (), s32[]{:S(2)}) async-start(), calls=%async_computation.13 | async-start | bytes 1474560 | tf_op jit(solution)/shard_map/reduce_scatter | solution.py:246
  336.9 209.1 %reduce-scatter.9.cloned.1.call-start = ((), (), s32[]{:S(2)}) async-start(), calls=%async_computation.12 | async-start | bytes 3932160 | tf_op jit(solution)/shard_map/reduce_scatter | solution.py:286
  346.4 6.5 copy-start.56
  353.0 3.2 copy-start.12
  353.0 3.2 copy-start.14
  357.6 7.2 copy-start.2
  364.8 2.8 copy-start.21
  364.8 3.4 copy-start.5
  374.1 11.0 %copy-start.7 = (bf16[1,512,192]{1,2,0:T(8,128)(2,1)S(1)}, bf16[1,512,192]{1,2,0:T(8,128)(2,1)}, u32[]{:S(2)}) copy-start(bf16[1,512,192]{1,2,0:T(8,128)(2,1)} %get-tuple-element.620) | copy-start | bytes 589828 | tf_op jit(solution)/shard_map/while
  374.1 11.0 %copy-start.9 = (bf16[1,512,192]{1,2,0:T(8,128)(2,1)S(1)}, bf16[1,512,192]{1,2,0:T(8,128)(2,1)}, u32[]{:S(2)}) copy-start(bf16[1,512,192]{1,2,0:T(8,128)(2,1)} %get-tuple-element.621) | copy-start | bytes 589828 | tf_op jit(solution)/shard_map/while
  385.9 1.5 copy-start.13
  385.9 1.6 copy-start.17
  387.5 3.1 copy-start.12
  387.5 3.1 copy-start.14
  392.0 7.2 copy-start.2
  399.2 2.8 copy-start.21
  399.3 3.4 copy-start.5
  408.5 11.0 %copy-start.7 = (bf16[1,512,192]{1,2,0:T(8,128)(2,1)S(1)}, bf16[1,512,192]{1,2,0:T(8,128)(2,1)}, u32[]{:S(2)}) copy-start(bf16[1,512,192]{1,2,0:T(8,128)(2,1)} %get-tuple-element.620) | copy-start | bytes 589828 | tf_op jit(solution)/shard_map/while
  408.5 11.0 %copy-start.9 = (bf16[1,512,192]{1,2,0:T(8,128)(2,1)S(1)}, bf16[1,512,192]{1,2,0:T(8,128)(2,1)}, u32[]{:S(2)}) copy-start(bf16[1,512,192]{1,2,0:T(8,128)(2,1)} %get-tuple-element.621) | copy-start | bytes 589828 | tf_op jit(solution)/shard_map/while
  420.3 1.5 copy-start.13
  420.4 1.5 copy-start.15
  420.4 1.6 copy-start.17
  422.2 2.5 copy-start.26
  422.2 2.6 copy-start.34
  429.7 277.8 %all-reduce.6.cloned.1.call-start = ((), (), s32[]{:S(2)}) async-start(), calls=%async_computation.14 | async-start | bytes 12976128 | tf_op jit(solution)/shard_map/psum | solution.py:291
  429.8 7.1 copy-start.52
  429.8 7.1 copy-start.59
  436.9 4.2 copy-start.11
  446.0 41.4 %copy-start.25 = (bf16[2,1024,192]{1,2,0:T(8,128)(2,1)S(1)}, bf16[2,1024,192]{1,2,0:T(8,128)(2,1)}, u32[]{:S(2)}) copy-start(bf16[2,1024,192]{1,2,0:T(8,128)(2,1)} %get-tuple-element.262) | copy-start | bytes 2359300
  446.0 41.6 %copy-start.49 = (f32[768]{0:T(1024)S(1)}, f32[768]{0:T(1024)}, u32[]{:S(2)}) copy-start(f32[768]{0:T(1024)} %get-tuple-element.410) | copy-start | bytes 9220
  446.1 99.9 %copy-start.23 = (f32[512,768]{1,0:T(8,128)S(1)}, f32[512,768]{1,0:T(8,128)}, u32[]{:S(2)}) copy-start(f32[512,768]{1,0:T(8,128)} %copy-done.22) | copy-start | bytes 4718596
  707.5 6.1 copy-start.32
  711.5 3.5 copy-start.31
  713.6 2.8 copy-start.1
  (28 other events, 29.2 us)
Sparse Core Ops, SparseCore 0:
  9.6 31.2 all-gather.4
  42.4 17.4 all-gather.6
  97.2 28.5 all-gather.8
  150.5 58.3 reduce-scatter.4
  217.3 28.5 all-gather.10
  263.2 58.3 reduce-scatter.6
  337.0 27.0 reduce-scatter.10
  429.8 38.7 reduce-scatter.8
  474.7 232.7 all-reduce.5
where the time goes:
time: 733 us; the launch traced here: 723 us
  waiting for transfers between devices  377 us (51%)
  matrix products  102 us (14%)
  blocking collectives  98.8 us (13%)
  local copies, waits for them, and re-layouts  78.3 us (11%)
  other arithmetic  40.3 us (5%)
  between operations  14.7 us (2%)
  starting transfers between devices  8.69 us (1%)
    psum x1, waiting for transfers between devices, body(): lax.psum((grad_w_query, grad_b_query, grad_w_key, grad_w_value, grad_b_va...  159 us
    reduce_scatter x1, waiting for transfers between devices, body(): lax.psum_scatter(contract_cols(grad_inner, w_inner), 'heads', scatter_dim...  58.5 us
    psum x1, blocking collectives, body(): lax.psum((grad_w_query, grad_b_query, grad_w_key, grad_w_value, grad_b_va...  58.3 us
    reduce_scatter x1, waiting for transfers between devices, body(): lax.psum_scatter(matmul(active, w_outer), 'heads', scatter_dimension=0, t...  54.6 us
    psum x1, blocking collectives, body(): lax.psum((grad_b_output, grad_gain1, grad_shift1, grad_b_outer, grad_gain...  40.5 us
    dot_general x6, matrix products, matmul(): return jnp.dot(left, right, preferred_element_type=jnp.float32)  30.5 us
    all_gather x1, waiting for transfers between devices, body(): full_tokens = lax.all_gather(tokens_in, 'heads', axis=0, tiled=True)  29.4 us
    all_gather x1, waiting for transfers between devices, body(): lax.all_gather(grad_two.astype(jnp.bfloat16), 'heads', axis=0, tiled=True)  28.5 us
  transfers between devices with their start and end apart: 11, of which 8 were waited for; matrix products, arithmetic and copies ran while one was open for 20% of the time, Pallas kernels for 0%

commit v1 on v0

v1 whole, which is shorter than its diff:
```python
import functools

import jax
import jax.numpy as jnp
from jax import lax
from jax.experimental import pallas as pl
from jax.experimental.pallas import tpu as pltpu
from jax.sharding import PartitionSpec as P

HEAD_DIM = 64
HALF = 1024
SCALE = HEAD_DIM ** (-0.5)
epsilon = 1e-06

bf16 = jnp.bfloat16
f32 = jnp.float32


def dot_nn(left, right):
    return jnp.dot(left, right, preferred_element_type=f32)


def dot_nt(left, right):
    return lax.dot_general(left, right, (((1,), (1,)), ((), ())), preferred_element_type=f32)


def dot_tn(left, right):
    return lax.dot_general(left, right, (((0,), (0,)), ((), ())), preferred_element_type=f32)


def swap(value, axis, stride):
    size = lax.axis_size(axis)
    return lax.ppermute(value, axis, [(i, i ^ stride) for i in range(size)])


def piece(value, index, axis):
    half = value.shape[axis] // 2
    return lax.dynamic_slice_in_dim(value, index * half, half, axis)


def ordered(mine, other, bit, axis):
    return jnp.where(
        bit == 0,
        jnp.concatenate([mine, other], axis=axis),
        jnp.concatenate([other, mine], axis=axis),
    )


def gather_halves(block, axis):
    y_bit = lax.axis_index("batch") & 1
    first = swap(piece(block, y_bit, axis), "heads", 2)
    second = swap(first, "batch", 1)
    return first, second


def norm_rows(hidden, gain, shift):
    center = jnp.mean(hidden, axis=1, keepdims=True)
    rinv = lax.rsqrt(jnp.mean(hidden * hidden, axis=1, keepdims=True) - center * center + epsilon)
    zhat = (hidden - center) * rinv
    return (zhat * gain + shift, zhat, rinv)


def norm_back(grad_zhat, zhat, rinv):
    first_mean = jnp.mean(grad_zhat, axis=1, keepdims=True)
    second_mean = jnp.mean(grad_zhat * zhat, axis=1, keepdims=True)
    return rinv * (grad_zhat - first_mean - zhat * second_mean)


def gelu_parts(values):
    cdf = 0.5 * lax.erfc(-values * 0.7071067811865476)
    density = jnp.exp(-0.5 * values * values) * 0.3989422804014327
    return values * cdf, cdf + values * density


def attend_blocks(flags, visit):
    heads = 3

    @pl.when(flags[0] == 1)
    def _():
        for block in range(2):
            for head in range(heads):
                visit(head, block * 512, (block ^ flags[1 + head]) * 512, 512)

    @pl.when(flags[0] == 0)
    def _():
        for block in range(4):
            for head in range(heads):
                visit(head, block * 256, (block ^ flags[1 + head]) * 256, 256)


def attend_forward_kernel(flags, q_ref, k_ref, v_ref, out_ref, lse_ref):
    def visit(head, q_at, k_at, size):
        cols = slice(head * HEAD_DIM, (head + 1) * HEAD_DIM)
        q_rows = pl.ds(q_at, size)
        k_rows = pl.ds(pl.multiple_of(k_at, 256), size)
        queries = q_ref[q_rows, cols] * SCALE
        keys = k_ref[k_rows, cols]
        values_t = v_ref[k_rows, cols].astype(f32).T.astype(bf16)
        scores_t = dot_nt(keys, queries.astype(bf16))
        top = jnp.max(scores_t, axis=0, keepdims=True)
        weights_t = jnp.exp(scores_t - top)
        total = jnp.sum(weights_t, axis=0, keepdims=True)
        mixed_t = dot_nn(values_t, weights_t.astype(bf16)) * (1.0 / total)
        out_ref[q_rows, cols] = mixed_t.T.astype(bf16)
        lse_ref[head : head + 1, q_rows] = top + jnp.log(total)

    attend_blocks(flags, visit)


def attend_backward_kernel(flags, q_ref, k_ref, v_ref, g_ref, lse_ref, dq_ref, dk_ref, dv_ref):
    def visit(head, q_at, k_at, size):
        cols = slice(head * HEAD_DIM, (head + 1) * HEAD_DIM)
        q_rows = pl.ds(q_at, size)
        k_rows = pl.ds(pl.multiple_of(k_at, 256), size)
        queries = (q_ref[q_rows, cols] * SCALE).astype(bf16)
        keys = k_ref[k_rows, cols]
        keys_t = keys.astype(f32).T.astype(bf16)
        grads = g_ref[q_rows, cols]
        scores_t = dot_nt(keys, queries)
        weights_t = jnp.exp(scores_t - lse_ref[head : head + 1, q_rows])
        grad_weights_t = dot_nt(v_ref[k_rows, cols], grads)
        delta = jnp.sum(weights_t * grad_weights_t, axis=0, keepdims=True)
        grad_scores_t = (weights_t * (grad_weights_t - delta)).astype(bf16)
        dv_ref[k_rows, cols] = dot_nn(weights_t.astype(bf16), grads).astype(bf16)
        dk_ref[k_rows, cols] = dot_nn(grad_scores_t, queries).astype(bf16)
        dq_ref[q_rows, cols] = (dot_nn(keys_t, grad_scores_t).T * SCALE).astype(bf16)

    attend_blocks(flags, visit)


VMEM_SPEC = pl.BlockSpec(memory_space=pltpu.VMEM)
SMEM_SPEC = pl.BlockSpec(memory_space=pltpu.SMEM)


def attend_forward(flags, queries, keys, values):
    rows, width = queries.shape
    pairs = rows * rows // 2 * (width // HEAD_DIM)
    return pl.pallas_call(
        attend_forward_kernel,
        out_shape=(
            jax.ShapeDtypeStruct((rows, width), bf16),
            jax.ShapeDtypeStruct((8, rows), f32),
        ),
        in_specs=[SMEM_SPEC] + [VMEM_SPEC] * 3,
        out_specs=(VMEM_SPEC, VMEM_SPEC),
        compiler_params=pltpu.CompilerParams(vmem_limit_bytes=32 * 1024 * 1024),
        cost_estimate=pl.CostEstimate(
            flops=pairs * 256 * 4, bytes_accessed=rows * width * 8, transcendentals=pairs
        ),
    )(flags, queries, keys, values)


def attend_backward(flags, queries, keys, values, grads, lse):
    rows, width = queries.shape
    pairs = rows * rows // 2 * (width // HEAD_DIM)
    return pl.pallas_call(
        attend_backward_kernel,
        out_shape=(jax.ShapeDtypeStruct((rows, width), bf16),) * 3,
        in_specs=[SMEM_SPEC] + [VMEM_SPEC] * 5,
        out_specs=(VMEM_SPEC,) * 3,
        compiler_params=pltpu.CompilerParams(vmem_limit_bytes=32 * 1024 * 1024),
        cost_estimate=pl.CostEstimate(
            flops=pairs * 256 * 10, bytes_accessed=rows * width * 14, transcendentals=pairs
        ),
    )(flags, queries, keys, values, grads, lse)


def reduce_gradient(own, partner_keep, partner_send, axis):
    index = lax.axis_index("batch")
    size = lax.axis_size("batch")
    y_bit = index & 1
    got_send = swap(partner_send, "heads", 2)
    got_keep = swap(partner_keep, "heads", 2)
    send = (piece(own, 1 - y_bit, axis).astype(f32) + got_send.astype(f32)).astype(bf16)
    got = swap(send, "batch", 1)
    total = piece(own, y_bit, axis).astype(f32) + got_keep.astype(f32) + got.astype(f32)
    stride = 2
    while stride < size:
        bit = (index // stride) & 1
        got = swap(piece(total, 1 - bit, 0).astype(bf16), "batch", stride)
        total = piece(total, bit, 0) + got.astype(f32)
        stride *= 2
    whole = total.astype(bf16)
    while stride > 2:
        stride //= 2
        bit = (index // stride) & 1
        whole = ordered(whole, swap(whole, "batch", stride), bit, 0)
    return ordered(whole, swap(whole, "batch", 1), y_bit, axis).astype(f32)


def body(
    tokens_in,
    cotangent,
    half_length,
    block_perm,
    w_query,
    b_query,
    w_key,
    w_value,
    b_value,
    w_output,
    b_output,
    norm1_gain,
    norm1_shift,
    w_inner,
    b_inner,
    w_outer,
    b_outer,
    norm2_gain,
    norm2_shift,
):
    width = w_query.shape[0]
    model = w_query.shape[1]
    units = w_outer.shape[0]
    rows = tokens_in.shape[0]
    head_count = width // HEAD_DIM
    hid = lax.axis_index("heads")
    y_bit = lax.axis_index("batch") & 1
    is_long = (half_length[hid // 2] == HALF).astype(jnp.int32)

    def flags_of(owner):
        swaps = lax.dynamic_slice_in_dim(block_perm[:, 0], owner * head_count, head_count)
        return jnp.concatenate([is_long[None], swaps])

    other_tokens = swap(tokens_in, "heads", 1)
    packed_bias = jnp.concatenate(
        [
            jnp.concatenate([b_query, b_value, jnp.zeros((model - 2 * width,), bf16)])[None],
            b_inner[None],
            jnp.zeros((30, model), bf16),
        ]
    )
    qkv_weights = jnp.concatenate([w_query, w_key, w_value], axis=0)
    packed = jnp.concatenate([qkv_weights, packed_bias], axis=0)
    first, second = gather_halves(packed, 0)
    packed_x = ordered(first, second, y_bit, 0)
    w_output_x = swap(w_output, "heads", 2)
    inner_x = gather_halves(w_inner, 1)
    outer_x = gather_halves(w_outer, 0)
    w_output_mine = jnp.concatenate([w_output, w_output_x], axis=0)
    w_output_other = swap(w_output_mine, "heads", 1)

    qkv_weights_x = packed_x[: 3 * width]
    bias_x = packed_x[3 * width]
    b_inner_x = packed_x[3 * width + 1]
    b_inner_x = jnp.where(y_bit == 0, b_inner_x, jnp.roll(b_inner_x, units // 2))
    parts = (
        (qkv_weights, b_query, b_value, flags_of(hid)),
        (qkv_weights_x, bias_x[:width], bias_x[width : 2 * width], flags_of(hid ^ 2)),
    )
    ffn_parts = (
        (w_inner, b_inner, w_outer),
        (inner_x[0], b_inner_x[: units // 2], outer_x[0]),
        (inner_x[1], b_inner_x[units // 2 :], outer_x[1]),
    )

    tokens = jnp.concatenate([tokens_in, other_tokens], axis=0)
    kept = []
    for weights, bias_q, bias_v, flags in parts:
        projected = dot_nt(tokens, weights)
        queries = (projected[:, :width] + bias_q.astype(f32)).astype(bf16)
        keys = projected[:, width : 2 * width].astype(bf16)
        values = (projected[:, 2 * width :] + bias_v.astype(f32)).astype(bf16)
        mixed, lse = attend_forward(flags, queries, keys, values)
        kept.append((queries, keys, values, lse, mixed))
    attended = jnp.concatenate([kept[0][4], kept[1][4]], axis=1)
    other_attended = swap(attended[rows:], "heads", 1)
    projected = dot_nn(attended[:rows], w_output_mine) + dot_nn(other_attended, w_output_other)
    hidden_one = tokens_in.astype(f32) + projected + b_output.astype(f32)
    gain1 = norm1_gain.astype(f32)
    gain2 = norm2_gain.astype(f32)
    normed, zhat_one, rinv_one = norm_rows(hidden_one, gain1, norm1_shift.astype(f32))

    normed_bf = normed.astype(bf16)
    normed_all = jnp.concatenate([normed_bf, swap(normed_bf, "heads", 1)], axis=0)
    ffn = None
    active = []
    slopes = []
    for inner_w, inner_b, outer_w in ffn_parts:
        inner = dot_nn(normed_all, inner_w) + inner_b.astype(f32)
        value, slope = gelu_parts(inner)
        active.append(value.astype(bf16))
        slopes.append(slope.astype(bf16))
        term = dot_nn(active[-1], outer_w)
        ffn = term if ffn is None else ffn + term
    other_ffn = swap(ffn[rows:].astype(bf16), "heads", 1)
    hidden_two = normed + ffn[:rows] + other_ffn.astype(f32) + b_outer.astype(f32)
    result, zhat_two, rinv_two = norm_rows(hidden_two, gain2, norm2_shift.astype(f32))
    block_out = result.astype(bf16)

    grad_out = cotangent.astype(f32)
    grad_gain2 = jnp.sum(grad_out * zhat_two, axis=0)
    grad_shift2 = jnp.sum(grad_out, axis=0)
    grad_two = norm_back(grad_out * gain2, zhat_two, rinv_two)
    grad_b_outer = jnp.sum(grad_two, axis=0)
    grad_two_bf = grad_two.astype(bf16)
    grad_two_all = jnp.concatenate([grad_two_bf, swap(grad_two_bf, "heads", 1)], axis=0)

    outer_grads = [dot_tn(active[i], grad_two_all).astype(bf16) for i in (2, 1, 0)][::-1]
    grad_w_outer = reduce_gradient(outer_grads[0], outer_grads[1], outer_grads[2], 0)

    grad_inner = []
    for i in range(3):
        grad_active = dot_nt(grad_two_all, ffn_parts[i][2])
        grad_inner.append((grad_active * slopes[i].astype(f32)).astype(bf16))
    inner_grads = [dot_tn(normed_all, grad_inner[i]).astype(bf16) for i in (2, 1, 0)][::-1]
    grad_w_inner = reduce_gradient(inner_grads[0], inner_grads[1], inner_grads[2], 1)
    inner_sums = [jnp.sum(grad_inner[i], axis=0, dtype=f32) for i in range(3)]
    back = sum(dot_nt(grad_inner[i], ffn_parts[i][0]) for i in range(3))
    other_back = swap(back[rows:].astype(bf16), "heads", 1)
    grad_normed = grad_two + back[:rows] + other_back.astype(f32)

    grad_gain1 = jnp.sum(grad_normed * zhat_one, axis=0)
    grad_shift1 = jnp.sum(grad_normed, axis=0)
    grad_one = norm_back(grad_normed * gain1, zhat_one, rinv_one)
    grad_b_output = jnp.sum(grad_one, axis=0)
    grad_one_bf = grad_one.astype(bf16)
    grad_one_all = jnp.concatenate([grad_one_bf, swap(grad_one_bf, "heads", 1)], axis=0)

    grad_attended = dot_nt(grad_one_all, w_output_mine).astype(bf16)
    grad_w_output = dot_tn(attended, grad_one_all).astype(bf16)
    grad_rows = []
    for number, (weights, bias_q, bias_v, flags) in enumerate(parts):
        queries, keys, values, lse, _ = kept[number]
        grads = grad_attended[:, number * width : (number + 1) * width]
        grad_rows.append(
            jnp.concatenate(attend_backward(flags, queries, keys, values, grads, lse), axis=1)
        )
    attn_grads = [
        jnp.concatenate(
            [
                grad_w_output[number * width : (number + 1) * width],
                dot_tn(grad_rows[number], tokens).astype(bf16),
            ],
            axis=0,
        )
        for number in range(2)
    ]
    grad_attn = reduce_gradient(
        attn_grads[0],
        piece(attn_grads[1], y_bit, 0),
        piece(attn_grads[1], 1 - y_bit, 0),
        0,
    )
    qkv_sums = [jnp.sum(grad_rows[i], axis=0, dtype=f32) for i in range(2)]

    input_terms = dot_nn(grad_rows[0], qkv_weights) + dot_nn(grad_rows[1], qkv_weights_x)
    other_terms = swap(input_terms[rows:].astype(bf16), "heads", 1)
    grad_tokens = grad_one + input_terms[:rows] + other_terms.astype(f32)

    row_sums = jnp.stack(
        [grad_b_output, grad_gain1, grad_shift1, grad_b_outer, grad_gain2, grad_shift2]
    )
    row_sums = row_sums + swap(row_sums, "heads", 1)
    inner_sum_x = jnp.concatenate(inner_sums[1:])
    inner_sum_x = jnp.where(y_bit == 0, inner_sum_x, jnp.roll(inner_sum_x, units // 2))
    vectors = jnp.concatenate([row_sums.reshape(-1), inner_sums[0], qkv_sums[0]])
    vectors_x = jnp.concatenate([row_sums.reshape(-1), inner_sum_x, qkv_sums[1]])
    vectors = vectors + swap(vectors_x, "heads", 2)
    stride = 1
    while stride < lax.axis_size("batch"):
        vectors = vectors + swap(vectors, "batch", stride)
        stride *= 2
    row_sums = vectors[: 6 * model].reshape(6, model)
    grad_b_inner = vectors[6 * model : 6 * model + units]
    qkv_sum = vectors[6 * model + units :]

    return (
        block_out,
        grad_tokens,
        grad_attn[width : 2 * width],
        qkv_sum[:width],
        grad_attn[2 * width : 3 * width],
        grad_attn[3 * width :],
        qkv_sum[2 * width :],
        grad_attn[:width],
        row_sums[0],
        row_sums[1],
        row_sums[2],
        grad_w_inner,
        grad_b_inner,
        grad_w_outer,
        row_sums[3],
        row_sums[4],
        row_sums[5],
    )


def solution(mesh):
    placed = (
        P(("batch", "heads"), None),
        P(("batch", "heads"), None),
        P("batch"),
        P(),
        P("heads", None),
        P("heads"),
        P("heads", None),
        P("heads", None),
        P("heads"),
        P("heads", None),
        P(),
        P(),
        P(),
        P(None, "heads"),
        P("heads"),
        P("heads", None),
        P(),
        P(),
        P(),
    )
    return jax.shard_map(
        body,
        mesh=mesh,
        in_specs=placed,
        out_specs=(
            P(("batch", "heads"), None),
            P(("batch", "heads"), None),
            P("heads", None),
            P("heads"),
            P("heads", None),
            P("heads", None),
            P("heads"),
            P("heads", None),
            P(),
            P(),
            P(),
            P(None, "heads"),
            P("heads"),
            P("heads", None),
            P(),
            P(),
            P(),
        ),
        check_vma=False,
    )
```

time: 733 us -> 353 us (0.48)
  waiting for transfers between devices: 377 us -> 135 us
  blocking collectives: 98.8 us -> 0 us
  local copies, waits for them, and re-layouts: 78.3 us -> 36.8 us
  starting transfers between devices: 8.69 us -> 47.2 us
  matrix products: 102 us -> 67 us
  Pallas kernels: 0 us -> 29.4 us
  between operations: 14.7 us -> 2.76 us
  other arithmetic: 40.3 us -> 30.3 us
    psum x1 -> x0, waiting for transfers between devices: 159 us -> none  [body(): lax.psum((grad_w_query, grad_b_query, grad_w_key, grad_w_value, grad_b_va...]
    ppermute x0 -> x45, waiting for transfers between devices: none -> 135 us  [swap(): return lax.ppermute(value, axis, [(i, i ^ stride) for i in range(size)])]
    reduce_scatter x4 -> x0, waiting for transfers between devices: 113 us -> none  [the longest x1 58.5 us: body(): lax.psum_scatter(contract_cols(grad_inner, w_inner), 'heads', scatter_dim...]
    psum x2 -> x0, blocking collectives: 98.8 us -> none  [the longest x1 58.3 us: body(): lax.psum((grad_w_query, grad_b_query, grad_w_key, grad_w_value, grad_b_va...]
    all_gather x4 -> x0, waiting for transfers between devices: 84.8 us -> none  [the longest x1 29.4 us: body(): full_tokens = lax.all_gather(tokens_in, 'heads', axis=0, tiled=True)]
    ppermute x0 -> x45, starting transfers between devices: none -> 47.2 us  [swap(): return lax.ppermute(value, axis, [(i, i ^ stride) for i in range(size)])]
    dot_general x46 -> x28, matrix products: 102 us -> 67 us  [the longest x10 32.7 us: dot_nn(): return jnp.dot(left, right, preferred_element_type=f32)]
    pallas_call x0 -> x4, Pallas kernels: none -> 29.4 us  [the longest x2 18.1 us: attend_forward(): pl.pallas_call(attend_forward_kernel, out_shape=(jax.ShapeDtypeStruct((ro...]
  transfers between devices with their start and end apart: 11 -> 45, of which waited for: 8 -> 21; matrix products, arithmetic and copies ran while one was open for 20% -> 31% of each run, Pallas kernels for 0% -> 8%
where the time goes in v1:
time: 353 us; the launch traced here: 348 us
  waiting for transfers between devices  135 us (38%)
  matrix products  67 us (19%)
  starting transfers between devices  47.2 us (13%)
  local copies, waits for them, and re-layouts  36.8 us (10%)
  other arithmetic  30.3 us (9%)
  Pallas kernels  29.4 us (8%)
    ppermute x45, waiting for transfers between devices, swap(): return lax.ppermute(value, axis, [(i, i ^ stride) for i in range(size)])  135 us
    ppermute x45, starting transfers between devices, swap(): return lax.ppermute(value, axis, [(i, i ^ stride) for i in range(size)])  47.2 us
    dot_general x10, matrix products, dot_nn(): return jnp.dot(left, right, preferred_element_type=f32)  32.7 us
    unnamed x138, local copies, waits for them, and re-layouts  19.3 us
    pallas_call x2, Pallas kernels, attend_forward(): pl.pallas_call(attend_forward_kernel, out_shape=(jax.ShapeDtypeStruct((ro...  18.1 us
    dot_general x9, matrix products, dot_tn(): lax.dot_general(left, right, (((0,), (0,)), ((), ())), preferred_element_...  17.5 us
    dot_general x9, matrix products, dot_nt(): lax.dot_general(left, right, (((1,), (1,)), ((), ())), preferred_element_...  16.9 us
    pallas_call x2, Pallas kernels, attend_backward(): pl.pallas_call(attend_backward_kernel, out_shape=(jax.ShapeDtypeStruct((r...  11.3 us
  transfers between devices with their start and end apart: 45, of which 21 were waited for; matrix products, arithmetic and copies ran while one was open for 31% of the time, Pallas kernels for 8%

profile of v1, /device:TPU:0, one launch (start us, length us, event | category | flops | bytes accessed | tf_op | source)
XLA Modules:
  0.0 348.3 jit_solution(9200826338864619408)
XLA Ops:
  2.3 5.7 %concatenate.128 = bf16[608,768]{1,0:T(8,128)(2,1)S(1)} concatenate(bf16[192,768]{1,0:T(8,128)(2,1)} %param.23, bf16[192,768]{1,0:T(8,128)(2,1)} %param.25, bf16[192,768]{1,0:T(8,128)(2,1)} %param.26, bf16[1,768]{1,0:T(2,128)(2,1)S(1)} %broadcast_in_dim.9, bf16[1,768]{1,0:T(2,128)(2,1)S(1)} %broadcast_in_dim.10, bf16[30,768]{1,0:T(8,128)(2,1)S(1)} %broadcast_in_dim.11), dimensions={0} | concatenate | bytes 1867776 | tf_op jit(solution)/shard_map/concatenate | solution.py:234
  8.8 2.9 collective-permute-start.1
  14.0 1.7 constant_dynamic-update-slice_fusion.6
  15.7 1.7 constant_dynamic-update-slice_fusion.3
  18.3 10.7 %collective-permute-done.3 = bf16[192,768]{1,0:T(8,128)(2,1)S(1)} collective-permute-done((bf16[192,768]{1,0:T(8,128)(2,1)}, bf16[192,768]{1,0:T(8,128)(2,1)S(1)}, u32[]{:S(2)}, u32[]{:S(2)}) %collective-permute-start.3) | collective-permute-done | bytes 294944 | tf_op jit(solution)/shard_map/ppermute | solution.py:33
  29.7 1.8 collective-permute-start.2
  36.8 1.7 add_convert_fusion.6
  38.6 4.1 %shard_map.314 = (bf16[1024,192]{1,0:T(8,128)(2,1)S(1)}, f32[8,1024]{1,0:T(8,128)S(1)}) custom-call(s32[4]{0:T(128)S(1)} %get-tuple-element.107.flags, bf16[1024,192]{1,0:T(8,128)(2,1)S(1)} %get-tuple-element.110.q_ref, bf16[1024,192]{1,0:T(8,128)(2,1)S(1)} %copy.52.k_ref, bf16[1024,192]{1,0:T(8,128)(2,1)S(1)} %get-tuple-element.109.v_ref), custom_call_target="tpu_custom_call" | custom-call | flops 1610612736 | bytes 1572864 | tf_op jit(solution)/shard_map/pallas_call | solution.py:138
  43.2 1.8 maximum_select_fusion.3
  48.0 2.4 copy.54
  53.0 1.7 add_convert_fusion.4
  54.7 14.0 %shard_map.315 = (bf16[1024,192]{1,0:T(8,128)(2,1)S(1)}, f32[8,1024]{1,0:T(8,128)S(1)}) custom-call(s32[4]{0:T(128)S(1)} %get-tuple-element.108.flags, bf16[1024,192]{1,0:T(8,128)(2,1)S(1)} %get-tuple-element.112.q_ref, bf16[1024,192]{1,0:T(8,128)(2,1)S(1)} %copy.55.k_ref, bf16[1024,192]{1,0:T(8,128)(2,1)S(1)} %get-tuple-element.111.v_ref), custom_call_target="tpu_custom_call" | custom-call | flops 1610612736 | bytes 1572864 | tf_op jit(solution)/shard_map/pallas_call | solution.py:138
  69.8 2.0 collective-permute-start.7
  73.1 1.8 fusion.92
  74.8 2.0 fusion.75
  77.5 8.5 %collective-permute-done.7 = bf16[768,384]{1,0:T(8,128)(2,1)S(1)} collective-permute-done((bf16[768,384]{1,0:T(8,128)(2,1)S(1)}, bf16[768,384]{1,0:T(8,128)(2,1)S(1)}, u32[]{:S(2)}, u32[]{:S(2)}) %collective-permute-start.7) | collective-permute-done | bytes 589856 | tf_op jit(solution)/shard_map/ppermute | solution.py:33
  86.0 1.7 collective-permute-start.9
  87.7 10.7 %collective-permute-done.8 = bf16[384,768]{1,0:T(8,128)(2,1)S(1)} collective-permute-done((bf16[384,768]{1,0:T(8,128)(2,1)S(1)}, bf16[384,768]{1,0:T(8,128)(2,1)S(1)}, u32[]{:S(2)}, u32[]{:S(2)}) %collective-permute-start.8) | collective-permute-done | bytes 589856 | tf_op jit(solution)/shard_map/ppermute | solution.py:33
  101.5 9.5 %multiply_convert_fusion.1 = (bf16[1024,768]{1,0:T(8,128)(2,1)S(1)}, f32[1024,768]{1,0:T(8,128)}, f32[1024,768]{1,0:T(8,128)}) fusion(f32[768]{0:T(1024)S(1)} %convert_element_type.286, bf16[768,768]{1,0:T(8,128)(2,1)S(1)} %copy-done, bf16[512,768]{1,0:T(8,128)(2,1)S(1)} %collective-permute-done.6, bf16[512,768]{1,0:T(8,128)(2,1)S(1)} %fusion.50), kind=kOutput, calls=%fused_computation.13 | convolution fusion | flops 1263009792 | bytes 10619904 | tf_op jit(solution)/shard_map/dot_general | solution.py:20
  110.9 6.4 %multiply_convert_fusion.5 = (bf16[1024,384]{1,0:T(8,128)(2,1)S(1)}, f32[1024,384]{1,0:T(8,128)}, f32[1024,384]{1,0:T(8,128)}) fusion(f32[384]{0:T(512)S(1)} %get-tuple-element.92, bf16[768,384]{1,0:T(8,128)(2,1)S(1)} %collective-permute-done.7, bf16[512,768]{1,0:T(8,128)(2,1)S(1)} %collective-permute-done.6, bf16[512,768]{1,0:T(8,128)(2,1)S(1)} %fusion.50), kind=kOutput, calls=%fused_computation.96 | convolution fusion | flops 633077760 | bytes 6096384 | tf_op jit(solution)/shard_map/dot_general | solution.py:20
  117.3 6.8 %multiply_convert_fusion.4 = (bf16[1024,384]{1,0:T(8,128)(2,1)S(1)}, f32[1024,384]{1,0:T(8,128)}, f32[1024,384]{1,0:T(8,128)}) fusion(f32[384]{0:T(512)S(1)} %get-tuple-element.91, bf16[768,384]{1,0:T(8,128)(2,1)S(1)} %collective-permute-done.9, bf16[512,768]{1,0:T(8,128)(2,1)S(1)} %collective-permute-done.6, bf16[512,768]{1,0:T(8,128)(2,1)S(1)} %fusion.50), kind=kOutput, calls=%fused_computation.82 | convolution fusion | flops 633077760 | bytes 6096384 | tf_op jit(solution)/shard_map/dot_general | solution.py:20
  128.3 1.8 collective-permute-done.11
  135.6 2.5 collective-permute-done.12
  138.0 3.2 convolution_convert_fusion.6
  141.3 1.7 collective-permute-start.37
  143.0 2.2 convolution_convert_fusion.5
  145.8 2.6 convert_reduce_fusion.5
  148.5 1.8 convolution_convert_fusion.8
  151.8 2.5 convert_reduce_fusion.4
  157.6 3.3 convert_reduce_fusion
  166.1 2.8 convolution_convert_fusion
  172.0 22.8 %collective-permute-done.30 = bf16[768,384]{1,0:T(8,128)(2,1)S(1)} collective-permute-done((bf16[768,384]{1,0:T(8,128)(2,1)S(1)}, bf16[768,384]{1,0:T(8,128)(2,1)S(1)}, u32[]{:S(2)}, u32[]{:S(2)}) %collective-permute-start.30) | collective-permute-done | bytes 589856 | tf_op jit(solution)/shard_map/ppermute | solution.py:33
  197.2 1.6 fusion.78
  199.0 2.4 convert_element_type.309
  201.9 1.7 convert_add_fusion
  203.7 1.9 collective-permute-start.40
  205.6 5.1 %collective-permute-done.31 = bf16[768,384]{1,0:T(8,128)(2,1)} collective-permute-done((bf16[768,384]{1,0:T(8,128)(2,1)}, bf16[768,384]{1,0:T(8,128)(2,1)}, u32[]{:S(2)}, u32[]{:S(2)}) %collective-permute-start.31) | collective-permute-done | bytes 589856 | tf_op jit(solution)/shard_map/ppermute | solution.py:33
  212.2 1.8 collective-permute-start.32
  214.1 2.7 collective-permute-start.41
  216.8 6.0 %collective-permute-done.32 = bf16[384,384]{1,0:T(8,128)(2,1)S(1)} collective-permute-done((bf16[384,384]{1,0:T(8,128)(2,1)S(1)}, bf16[384,384]{1,0:T(8,128)(2,1)S(1)}, u32[]{:S(2)}, u32[]{:S(2)}) %collective-permute-start.32) | collective-permute-done | bytes 294944 | tf_op jit(solution)/shard_map/ppermute | solution.py:33
  222.8 1.9 collective-permute-start.33
  224.7 2.5 convolution_convert_fusion.4
  228.5 5.8 %shard_map.317 = (bf16[1024,192]{1,0:T(8,128)(2,1)S(1)}, bf16[1024,192]{1,0:T(8,128)(2,1)S(1)}, bf16[1024,192]{1,0:T(8,128)(2,1)S(1)}) custom-call(s32[4]{0:T(128)S(1)} %get-tuple-element.108.flags, bf16[1024,192]{1,0:T(8,128)(2,1)S(1)} %copy-done.8, bf16[1024,192]{1,0:T(8,128)(2,1)S(1)} %copy.55.k_ref, bf16[1024,192]{1,0:T(8,128)(2,1)S(1)} %copy-done.6, ...), custom_call_target="tpu_custom_call" | custom-call | flops 4026531840 | bytes 2752512 | tf_op jit(solution)/shard_map/pallas_call | solution.py:156
  237.4 2.3 convolution_convert_fusion.9
  240.5 1.7 collective-permute-start.17
  242.6 5.5 %shard_map.316 = (bf16[1024,192]{1,0:T(8,128)(2,1)S(1)}, bf16[1024,192]{1,0:T(8,128)(2,1)S(1)}, bf16[1024,192]{1,0:T(8,128)(2,1)S(1)}) custom-call(s32[4]{0:T(128)S(1)} %get-tuple-element.107.flags, bf16[1024,192]{1,0:T(8,128)(2,1)S(1)} %copy-done.4, bf16[1024,192]{1,0:T(8,128)(2,1)S(1)} %copy.52.k_ref, bf16[1024,192]{1,0:T(8,128)(2,1)S(1)} %copy-done.2, ...), custom_call_target="tpu_custom_call" | custom-call | flops 4026531840 | bytes 2752512 | tf_op jit(solution)/shard_map/pallas_call | solution.py:156
  252.1 4.8 %collective-permute-done.17 = bf16[384,768]{1,0:T(8,128)(2,1)S(1)} collective-permute-done((bf16[384,768]{1,0:T(8,128)(2,1)S(1)}, bf16[384,768]{1,0:T(8,128)(2,1)S(1)}, u32[]{:S(2)}, u32[]{:S(2)}) %collective-permute-start.17) | collective-permute-done | bytes 589856 | tf_op jit(solution)/shard_map/ppermute | solution.py:33
  261.0 6.5 %collective-permute-done.26 = f32[5952]{0:T(1024)S(1)} collective-permute-done((f32[5952]{0:T(1024)S(1)}, f32[5952]{0:T(1024)S(1)}, u32[]{:S(2)}, u32[]{:S(2)}) %collective-permute-start.26) | collective-permute-done | bytes 23840 | tf_op jit(solution)/shard_map/ppermute | solution.py:33
  267.5 2.5 collective-permute-start.27
  270.7 2.0 collective-permute-start.42
  274.0 1.8 collective-permute-start.34
  275.7 6.0 %collective-permute-done.28 = f32[5952]{0:T(1024)S(1)} collective-permute-done((f32[5952]{0:T(1024)S(1)}, f32[5952]{0:T(1024)S(1)}, u32[]{:S(2)}, u32[]{:S(2)}) %collective-permute-start.28) | collective-permute-done | bytes 23840 | tf_op jit(solution)/shard_map/ppermute | solution.py:33
  281.8 3.1 collective-permute-done.19
  286.1 8.4 %collective-permute-done.20 = bf16[96,768]{1,0:T(8,128)(2,1)S(1)} collective-permute-done((bf16[96,768]{1,0:T(8,128)(2,1)S(1)}, bf16[96,768]{1,0:T(8,128)(2,1)S(1)}, u32[]{:S(2)}, u32[]{:S(2)}) %collective-permute-start.20) | collective-permute-done | bytes 147488 | tf_op jit(solution)/shard_map/ppermute | solution.py:33
  294.7 2.0 collective-permute-start.43
  296.9 6.2 %collective-permute-done.21 = bf16[96,768]{1,0:T(8,128)(2,1)S(1)} collective-permute-done((bf16[96,768]{1,0:T(8,128)(2,1)S(1)}, bf16[96,768]{1,0:T(8,128)(2,1)S(1)}, u32[]{:S(2)}, u32[]{:S(2)}) %collective-permute-start.21) | collective-permute-done | bytes 147488 | tf_op jit(solution)/shard_map/ppermute | solution.py:33
  303.9 3.9 %collective-permute-done.43 = bf16[192,768]{1,0:T(8,128)(2,1)S(1)} collective-permute-done((bf16[192,768]{1,0:T(8,128)(2,1)S(1)}, bf16[192,768]{1,0:T(8,128)(2,1)S(1)}, u32[]{:S(2)}, u32[]{:S(2)}) %collective-permute-start.43) | collective-permute-done | bytes 294944 | tf_op jit(solution)/shard_map/ppermute | solution.py:33
  308.0 2.1 collective-permute-start.44
  310.0 4.1 %collective-permute-done.35 = bf16[384,384]{1,0:T(8,128)(2,1)S(1)} collective-permute-done((bf16[384,384]{1,0:T(8,128)(2,1)S(1)}, bf16[384,384]{1,0:T(8,128)(2,1)S(1)}, u32[]{:S(2)}, u32[]{:S(2)}) %collective-permute-start.35) | collective-permute-done | bytes 294944 | tf_op jit(solution)/shard_map/ppermute | solution.py:33
  314.3 2.1 collective-permute-start.36
  316.3 2.9 collective-permute-done.22
  319.5 1.9 collective-permute-start.23
  325.9 11.0 %collective-permute-done.36 = bf16[768,384]{1,0:T(8,128)(2,1)S(1)} collective-permute-done((bf16[768,384]{1,0:T(8,128)(2,1)S(1)}, bf16[768,384]{1,0:T(8,128)(2,1)S(1)}, u32[]{:S(2)}, u32[]{:S(2)}) %collective-permute-start.36) | collective-permute-done | bytes 589856 | tf_op jit(solution)/shard_map/ppermute | solution.py:33
  338.6 7.8 %collective-permute-done.23 = bf16[384,768]{1,0:T(8,128)(2,1)S(1)} collective-permute-done((bf16[384,768]{1,0:T(8,128)(2,1)S(1)}, bf16[384,768]{1,0:T(8,128)(2,1)S(1)}, u32[]{:S(2)}, u32[]{:S(2)}) %collective-permute-start.23) | collective-permute-done | bytes 589856 | tf_op jit(solution)/shard_map/ppermute | solution.py:33
  (303 shorter events, 76.7 us)
Async XLA Ops:
  0.7 69.0 %copy-start = (bf16[768,768]{1,0:T(8,128)(2,1)S(1)}, bf16[768,768]{1,0:T(8,128)(2,1)}, u32[]{:S(2)}) copy-start(bf16[768,768]{1,0:T(8,128)(2,1)} %param.32) | copy-start | bytes 3538948
  0.7 11.3 %copy-start.19 = (bf16[192,768]{1,0:T(8,128)(2,1)S(1)}, bf16[192,768]{1,0:T(8,128)(2,1)}, u32[]{:S(2)}) copy-start(bf16[192,768]{1,0:T(8,128)(2,1)} %param.23) | copy-start | bytes 884740
  0.7 11.1 %copy-start.16 = (bf16[512,768]{1,0:T(8,128)(2,1)S(1)}, bf16[512,768]{1,0:T(8,128)(2,1)}, u32[]{:S(2)}) copy-start(bf16[512,768]{1,0:T(8,128)(2,1)} %param.19) | copy-start | bytes 2359300
  2.3 10.3 %copy-start.55 = (s32[2]{0:T(128)S(1)}, s32[2]{0:T(128)}, u32[]{:S(2)}) copy-start(s32[2]{0:T(128)} %param.21) | copy-start | bytes 28
  2.3 11.6 %slice-start = ((s32[12,2]{0,1:T(2,128)}), s32[12,1]{0,1:T(1,128)S(1)}, s32[]{:S(2)}) async-start(s32[12,2]{0,1:T(2,128)} %param.22), calls=%async_computation | async-start | bytes 1024 | tf_op jit(solution)/shard_map/slice | solution.py:222
  8.0 9.4 %copy-start.51 = (bf16[192]{0:T(256)(128)(2,1)S(1)}, bf16[192]{0:T(256)(128)(2,1)}, u32[]{:S(2)}) copy-start(bf16[192]{0:T(256)(128)(2,1)} %param.24) | copy-start | bytes 1156
  8.8 20.9 %collective-permute-start.1 = (bf16[304,768]{1,0:T(8,128)(2,1)}, bf16[304,768]{1,0:T(8,128)(2,1)}, u32[]{:S(2)}, u32[]{:S(2)}) collective-permute-start(bf16[304,768]{1,0:T(8,128)(2,1)} %constant_dynamic-slice_fusion.2), channel_id=1, source_target_pairs={{0,2},{1,3},{2,0},{3,1},{4,6},{5,7},{6,4},{7,5},{8,10},{9,11},{10,... | collective-permute-start | bytes 1400840 | tf_op jit(solution)/shard_map/ppermute | solution.py:33
  11.8 19.7 %collective-permute-start = (bf16[512,768]{1,0:T(8,128)(2,1)S(1)}, bf16[512,768]{1,0:T(8,128)(2,1)}, u32[]{:S(2)}, u32[]{:S(2)}) collective-permute-start(bf16[512,768]{1,0:T(8,128)(2,1)S(1)} %copy-done.16), channel_id=1, source_target_pairs={{0,1},{1,0},{2,3},{3,2},{4,5},{5,4},{6,7},{7,6},{8,9},{9,8},{10,11... | collective-permute-start | bytes 2359304 | tf_op jit(solution)/shard_map/ppermute | solution.py:33
  11.8 17.2 %collective-permute-start.3 = (bf16[192,768]{1,0:T(8,128)(2,1)}, bf16[192,768]{1,0:T(8,128)(2,1)S(1)}, u32[]{:S(2)}, u32[]{:S(2)}) collective-permute-start(bf16[192,768]{1,0:T(8,128)(2,1)} %param.28), channel_id=1, source_target_pairs={{0,2},{1,3},{2,0},{3,1},{4,6},{5,7},{6,4},{7,5},{8,10},{9,11},{10,... | collective-permute-start | bytes 884744 | tf_op jit(solution)/shard_map/ppermute | solution.py:33
  18.2 14.5 %copy-start.42 = (bf16[576,768]{1,0:T(8,128)(2,1)S(1)}, bf16[576,768]{1,0:T(8,128)(2,1)}, u32[]{:S(2)}) copy-start(bf16[576,768]{1,0:T(8,128)(2,1)} %constant_dynamic-update-slice_fusion.2) | copy-start | bytes 2654212
  29.7 43.3 %collective-permute-start.5 = (bf16[384,768]{1,0:T(8,128)(2,1)}, bf16[384,768]{1,0:T(8,128)(2,1)}, u32[]{:S(2)}, u32[]{:S(2)}) collective-permute-start(bf16[384,768]{1,0:T(8,128)(2,1)} %constant_dynamic-update-slice_fusion.5), channel_id=1, source_target_pairs={{0,1},{1,0},{2,3},{3,2},{4,5},{5,4},{6,7},{7,6},{8,9},{9,8},{10,11... | collective-permute-start | bytes 1769480 | tf_op jit(solution)/shard_map/ppermute | solution.py:33
  29.7 13.5 %collective-permute-start.2 = (bf16[304,768]{1,0:T(8,128)(2,1)}, bf16[304,768]{1,0:T(8,128)(2,1)}, u32[]{:S(2)}, u32[]{:S(2)}) collective-permute-start(bf16[304,768]{1,0:T(8,128)(2,1)} %collective-permute-done.1), channel_id=1, source_target_pairs={{0,4},{4,0},{8,12},{12,8},{16,20},{20,16},{24,28},{28,24},{1,5},{5... | collective-permute-start | bytes 1400840 | tf_op jit(solution)/shard_map/ppermute | solution.py:33
  54.7 14.0 %copy-start.5 = (bf16[1024,192]{1,0:T(8,128)(2,1)}, bf16[1024,192]{1,0:T(8,128)(2,1)S(1)}, u32[]{:S(2)}) copy-start(bf16[1024,192]{1,0:T(8,128)(2,1)S(1)} %get-tuple-element.111.v_ref) | copy-start | bytes 1179652
  54.7 14.0 %copy-start.7 = (bf16[1024,192]{1,0:T(8,128)(2,1)}, bf16[1024,192]{1,0:T(8,128)(2,1)S(1)}, u32[]{:S(2)}) copy-start(bf16[1024,192]{1,0:T(8,128)(2,1)S(1)} %get-tuple-element.112.q_ref) | copy-start | bytes 1179652
  69.7 3.4 collective-permute-start.4
  69.8 16.3 %collective-permute-start.7 = (bf16[768,384]{1,0:T(8,128)(2,1)S(1)}, bf16[768,384]{1,0:T(8,128)(2,1)S(1)}, u32[]{:S(2)}, u32[]{:S(2)}) collective-permute-start(bf16[768,384]{1,0:T(8,128)(2,1)S(1)} %constant_dynamic-slice_fusion.1), channel_id=1, source_target_pairs={{0,2},{1,3},{2,0},{3,1},{4,6},{5,7},{6,4},{7,5},{8,10},{9,11},{10,... | collective-permute-start | bytes 1769480 | tf_op jit(solution)/shard_map/ppermute | solution.py:33
  71.8 26.6 %collective-permute-start.8 = (bf16[384,768]{1,0:T(8,128)(2,1)S(1)}, bf16[384,768]{1,0:T(8,128)(2,1)S(1)}, u32[]{:S(2)}, u32[]{:S(2)}) collective-permute-start(bf16[384,768]{1,0:T(8,128)(2,1)S(1)} %constant_dynamic-slice_fusion), channel_id=1, source_target_pairs={{0,2},{1,3},{2,0},{3,1},{4,6},{5,7},{6,4},{7,5},{8,10},{9,11},{10,... | collective-permute-start | bytes 1769480 | tf_op jit(solution)/shard_map/ppermute | solution.py:33
  76.8 53.3 %copy-start.9 = (f32[512,768]{1,0:T(8,128)}, f32[512,768]{1,0:T(8,128)S(1)}, u32[]{:S(2)}) copy-start(f32[512,768]{1,0:T(8,128)S(1)} %get-tuple-element.97) | copy-start | bytes 4718596
  77.2 40.1 %copy-start.24 = (bf16[512,768]{1,0:T(8,128)(2,1)}, bf16[512,768]{1,0:T(8,128)(2,1)S(1)}, u32[]{:S(2)}) copy-start(bf16[512,768]{1,0:T(8,128)(2,1)S(1)} %fusion.50) | copy-start | bytes 2359300
  77.2 24.3 %collective-permute-start.6 = (bf16[512,768]{1,0:T(8,128)(2,1)S(1)}, bf16[512,768]{1,0:T(8,128)(2,1)S(1)}, u32[]{:S(2)}, u32[]{:S(2)}) collective-permute-start(bf16[512,768]{1,0:T(8,128)(2,1)S(1)} %fusion.50), channel_id=1, source_target_pairs={{0,1},{1,0},{2,3},{3,2},{4,5},{5,4},{6,7},{7,6},{8,9},{9,8},{10,11... | collective-permute-start | bytes 2359304 | tf_op jit(solution)/shard_map/ppermute | solution.py:33
  86.0 24.9 %copy-start.29 = (bf16[768,384]{1,0:T(8,128)(2,1)}, bf16[768,384]{1,0:T(8,128)(2,1)S(1)}, u32[]{:S(2)}) copy-start(bf16[768,384]{1,0:T(8,128)(2,1)S(1)} %collective-permute-done.7) | copy-start | bytes 1769476
  86.0 31.3 %collective-permute-start.9 = (bf16[768,384]{1,0:T(8,128)(2,1)S(1)}, bf16[768,384]{1,0:T(8,128)(2,1)S(1)}, u32[]{:S(2)}, u32[]{:S(2)}) collective-permute-start(bf16[768,384]{1,0:T(8,128)(2,1)S(1)} %collective-permute-done.7), channel_id=1, source_target_pairs={{0,4},{4,0},{8,12},{12,8},{16,20},{20,16},{24,28},{28,24},{1,5},{5... | collective-permute-start | bytes 1769480 | tf_op jit(solution)/shard_map/ppermute | solution.py:33
  98.4 25.8 %copy-start.31 = (bf16[384,768]{1,0:T(8,128)(2,1)}, bf16[384,768]{1,0:T(8,128)(2,1)S(1)}, u32[]{:S(2)}) copy-start(bf16[384,768]{1,0:T(8,128)(2,1)S(1)} %collective-permute-done.8) | copy-start | bytes 1769476
  98.4 28.2 %collective-permute-start.10 = (bf16[384,768]{1,0:T(8,128)(2,1)S(1)}, bf16[384,768]{1,0:T(8,128)(2,1)S(1)}, u32[]{:S(2)}, u32[]{:S(2)}) collective-permute-start(bf16[384,768]{1,0:T(8,128)(2,1)S(1)} %collective-permute-done.8), channel_id=1, source_target_pairs={{0,4},{4,0},{8,12},{12,8},{16,20},{20,16},{24,28},{28,24},{1,5},{5... | collective-permute-start | bytes 1769480 | tf_op jit(solution)/shard_map/ppermute | solution.py:33
  101.4 15.9 %copy-start.53 = (bf16[512,768]{1,0:T(8,128)(2,1)}, bf16[512,768]{1,0:T(8,128)(2,1)S(1)}, u32[]{:S(2)}) copy-start(bf16[512,768]{1,0:T(8,128)(2,1)S(1)} %collective-permute-done.6) | copy-start | bytes 2359300
  110.9 14.2 %copy-start.60 = (bf16[1024,768]{1,0:T(8,128)(2,1)}, bf16[1024,768]{1,0:T(8,128)(2,1)S(1)}, u32[]{:S(2)}) copy-start(bf16[1024,768]{1,0:T(8,128)(2,1)S(1)} %get-tuple-element.61) | copy-start | bytes 4718596
  127.7 2.4 collective-permute-start.11
  135.4 2.6 collective-permute-start.12
  141.3 60.6 %collective-permute-start.37 = (bf16[384,768]{1,0:T(8,128)(2,1)}, bf16[384,768]{1,0:T(8,128)(2,1)}, u32[]{:S(2)}, u32[]{:S(2)}) collective-permute-start(bf16[384,768]{1,0:T(8,128)(2,1)} %convolution_convert_fusion.6), channel_id=1, source_target_pairs={{0,2},{1,3},{2,0},{3,1},{4,6},{5,7},{6,4},{7,5},{8,10},{9,11},{10,... | collective-permute-start | bytes 1769480 | tf_op jit(solution)/shard_map/ppermute | solution.py:33
  145.2 25.3 %collective-permute-start.38 = (bf16[384,768]{1,0:T(8,128)(2,1)S(1)}, bf16[384,768]{1,0:T(8,128)(2,1)S(1)}, u32[]{:S(2)}, u32[]{:S(2)}) collective-permute-start(bf16[384,768]{1,0:T(8,128)(2,1)S(1)} %convolution_convert_fusion.5), channel_id=1, source_target_pairs={{0,2},{1,3},{2,0},{3,1},{4,6},{5,7},{6,4},{7,5},{8,10},{9,11},{10,... | collective-permute-start | bytes 1769480 | tf_op jit(solution)/shard_map/ppermute | solution.py:33
  150.3 55.3 %collective-permute-start.29 = (bf16[768,384]{1,0:T(8,128)(2,1)}, bf16[768,384]{1,0:T(8,128)(2,1)}, u32[]{:S(2)}, u32[]{:S(2)}) collective-permute-start(bf16[768,384]{1,0:T(8,128)(2,1)} %convolution_convert_fusion.8), channel_id=1, source_target_pairs={{0,2},{1,3},{2,0},{3,1},{4,6},{5,7},{6,4},{7,5},{8,10},{9,11},{10,... | collective-permute-start | bytes 1769480 | tf_op jit(solution)/shard_map/ppermute | solution.py:33
  155.4 39.4 %collective-permute-start.30 = (bf16[768,384]{1,0:T(8,128)(2,1)S(1)}, bf16[768,384]{1,0:T(8,128)(2,1)S(1)}, u32[]{:S(2)}, u32[]{:S(2)}) collective-permute-start(bf16[768,384]{1,0:T(8,128)(2,1)S(1)} %convolution_convert_fusion.7), channel_id=1, source_target_pairs={{0,2},{1,3},{2,0},{3,1},{4,6},{5,7},{6,4},{7,5},{8,10},{9,11},{10,... | collective-permute-start | bytes 1769480 | tf_op jit(solution)/shard_map/ppermute | solution.py:33
  164.8 31.5 %collective-permute-start.13 = (bf16[512,768]{1,0:T(8,128)(2,1)S(1)}, bf16[512,768]{1,0:T(8,128)(2,1)S(1)}, u32[]{:S(2)}, u32[]{:S(2)}) collective-permute-start(bf16[512,768]{1,0:T(8,128)(2,1)S(1)} %slice.284), channel_id=1, source_target_pairs={{0,1},{1,0},{2,3},{3,2},{4,5},{5,4},{6,7},{7,6},{8,9},{9,8},{10,11... | collective-permute-start | bytes 2359304 | tf_op jit(solution)/shard_map/ppermute | solution.py:33
  170.4 25.4 %copy-start.21 = (bf16[768,768]{1,0:T(8,128)(2,1)}, bf16[768,768]{1,0:T(8,128)(2,1)S(1)}, u32[]{:S(2)}) copy-start(bf16[768,768]{1,0:T(8,128)(2,1)S(1)} %convolution_convert_fusion.1) | copy-start | bytes 3538948
  170.4 25.8 %copy-start.10 = (f32[512,768]{1,0:T(8,128)S(1)}, f32[512,768]{1,0:T(8,128)}, u32[]{:S(2)}) copy-start(f32[512,768]{1,0:T(8,128)} %copy-done.9) | copy-start | bytes 4718596
  170.4 25.8 %copy-start.13 = (f32[512,768]{1,0:T(8,128)S(1)}, f32[512,768]{1,0:T(8,128)}, u32[]{:S(2)}) copy-start(f32[512,768]{1,0:T(8,128)} %copy-done.12) | copy-start | bytes 4718596
  171.5 30.5 %collective-permute-start.39 = (bf16[384,768]{1,0:T(8,128)(2,1)}, bf16[384,768]{1,0:T(8,128)(2,1)}, u32[]{:S(2)}, u32[]{:S(2)}) collective-permute-start(bf16[384,768]{1,0:T(8,128)(2,1)} %add_convert_fusion.1), channel_id=1, source_target_pairs={{0,4},{4,0},{8,12},{12,8},{16,20},{20,16},{24,28},{28,24},{1,5},{5... | collective-permute-start | bytes 1769480 | tf_op jit(solution)/shard_map/ppermute | solution.py:33
  195.8 14.9 %collective-permute-start.31 = (bf16[768,384]{1,0:T(8,128)(2,1)}, bf16[768,384]{1,0:T(8,128)(2,1)}, u32[]{:S(2)}, u32[]{:S(2)}) collective-permute-start(bf16[768,384]{1,0:T(8,128)(2,1)} %add_convert_fusion.2), channel_id=1, source_target_pairs={{0,4},{4,0},{8,12},{12,8},{16,20},{20,16},{24,28},{28,24},{1,5},{5... | collective-permute-start | bytes 1769480 | tf_op jit(solution)/shard_map/ppermute | solution.py:33
  198.9 2.5 collective-permute-start.24
  201.4 23.3 %collective-permute-start.14 = (bf16[512,768]{1,0:T(8,128)(2,1)}, bf16[512,768]{1,0:T(8,128)(2,1)}, u32[]{:S(2)}, u32[]{:S(2)}) collective-permute-start(bf16[512,768]{1,0:T(8,128)(2,1)} %convert_element_type.309), channel_id=1, source_target_pairs={{0,1},{1,0},{2,3},{3,2},{4,5},{5,4},{6,7},{7,6},{8,9},{9,8},{10,11... | collective-permute-start | bytes 2359304 | tf_op jit(solution)/shard_map/ppermute | solution.py:33
  203.7 10.3 %collective-permute-start.40 = (bf16[192,768]{1,0:T(8,128)(2,1)S(1)}, bf16[192,768]{1,0:T(8,128)(2,1)S(1)}, u32[]{:S(2)}, u32[]{:S(2)}) collective-permute-start(bf16[192,768]{1,0:T(8,128)(2,1)S(1)} %dynamic-slice_convert_fusion), channel_id=1, source_target_pairs={{0,8},{4,12},{8,0},{12,4},{16,24},{20,28},{24,16},{28,20},{1,9},{5... | collective-permute-start | bytes 884744 | tf_op jit(solution)/shard_map/ppermute | solution.py:33
  212.2 10.6 %collective-permute-start.32 = (bf16[384,384]{1,0:T(8,128)(2,1)S(1)}, bf16[384,384]{1,0:T(8,128)(2,1)S(1)}, u32[]{:S(2)}, u32[]{:S(2)}) collective-permute-start(bf16[384,384]{1,0:T(8,128)(2,1)S(1)} %dynamic-slice_convert_fusion.1), channel_id=1, source_target_pairs={{0,8},{4,12},{8,0},{12,4},{16,24},{20,28},{24,16},{28,20},{1,9},{5... | collective-permute-start | bytes 884744 | tf_op jit(solution)/shard_map/ppermute | solution.py:33
  214.1 56.5 %collective-permute-start.41 = (bf16[96,768]{1,0:T(8,128)(2,1)S(1)}, bf16[96,768]{1,0:T(8,128)(2,1)S(1)}, u32[]{:S(2)}, u32[]{:S(2)}) collective-permute-start(bf16[96,768]{1,0:T(8,128)(2,1)S(1)} %dynamic-slice_convert_fusion.3), channel_id=1, source_target_pairs={{0,16},{4,20},{8,24},{12,28},{16,0},{20,4},{24,8},{28,12},{1,17},{... | collective-permute-start | bytes 442376 | tf_op jit(solution)/shard_map/ppermute | solution.py:33
  222.8 51.1 %collective-permute-start.33 = (bf16[192,384]{1,0:T(8,128)(2,1)S(1)}, bf16[192,384]{1,0:T(8,128)(2,1)S(1)}, u32[]{:S(2)}, u32[]{:S(2)}) collective-permute-start(bf16[192,384]{1,0:T(8,128)(2,1)S(1)} %dynamic-slice_convert_fusion.4), channel_id=1, source_target_pairs={{0,16},{4,20},{8,24},{12,28},{16,0},{20,4},{24,8},{28,12},{1,17},{... | collective-permute-start | bytes 442376 | tf_op jit(solution)/shard_map/ppermute | solution.py:33
  237.0 21.4 %collective-permute-start.25 = (f32[5952]{0:T(1024)S(1)}, f32[5952]{0:T(1024)S(1)}, u32[]{:S(2)}, u32[]{:S(2)}) collective-permute-start(f32[5952]{0:T(1024)S(1)} %fusion.66), channel_id=1, source_target_pairs={{0,2},{1,3},{2,0},{3,1},{4,6},{5,7},{6,4},{7,5},{8,10},{9,11},{10,... | collective-permute-start | bytes 71432 | tf_op jit(solution)/shard_map/ppermute | solution.py:33
  240.5 16.3 %collective-permute-start.17 = (bf16[384,768]{1,0:T(8,128)(2,1)S(1)}, bf16[384,768]{1,0:T(8,128)(2,1)S(1)}, u32[]{:S(2)}, u32[]{:S(2)}) collective-permute-start(bf16[384,768]{1,0:T(8,128)(2,1)S(1)} %get-tuple-element.73), channel_id=1, source_target_pairs={{0,2},{1,3},{2,0},{3,1},{4,6},{5,7},{6,4},{7,5},{8,10},{9,11},{10,... | collective-permute-start | bytes 1769480 | tf_op jit(solution)/shard_map/ppermute | solution.py:33
  242.3 25.2 %collective-permute-start.16 = (bf16[384,768]{1,0:T(8,128)(2,1)S(1)}, bf16[384,768]{1,0:T(8,128)(2,1)S(1)}, u32[]{:S(2)}, u32[]{:S(2)}) collective-permute-start(bf16[384,768]{1,0:T(8,128)(2,1)S(1)} %get-tuple-element.72), channel_id=1, source_target_pairs={{0,2},{1,3},{2,0},{3,1},{4,6},{5,7},{6,4},{7,5},{8,10},{9,11},{10,... | collective-permute-start | bytes 1769480 | tf_op jit(solution)/shard_map/ppermute | solution.py:33
  257.3 12.8 %collective-permute-start.18 = (bf16[384,768]{1,0:T(8,128)(2,1)S(1)}, bf16[384,768]{1,0:T(8,128)(2,1)S(1)}, u32[]{:S(2)}, u32[]{:S(2)}) collective-permute-start(bf16[384,768]{1,0:T(8,128)(2,1)S(1)} %add_convert_fusion.3), channel_id=1, source_target_pairs={{0,4},{4,0},{8,12},{12,8},{16,20},{20,16},{24,28},{28,24},{1,5},{5... | collective-permute-start | bytes 1769480 | tf_op jit(solution)/shard_map/ppermute | solution.py:33
  258.4 9.1 %collective-permute-start.26 = (f32[5952]{0:T(1024)S(1)}, f32[5952]{0:T(1024)S(1)}, u32[]{:S(2)}, u32[]{:S(2)}) collective-permute-start(f32[5952]{0:T(1024)S(1)} %fusion.65), channel_id=1, source_target_pairs={{0,4},{4,0},{8,12},{12,8},{16,20},{20,16},{24,28},{28,24},{1,5},{5... | collective-permute-start | bytes 71432 | tf_op jit(solution)/shard_map/ppermute | solution.py:33
  267.5 53.9 %collective-permute-start.15 = (bf16[512,768]{1,0:T(8,128)(2,1)S(1)}, bf16[512,768]{1,0:T(8,128)(2,1)S(1)}, u32[]{:S(2)}, u32[]{:S(2)}) collective-permute-start(bf16[512,768]{1,0:T(8,128)(2,1)S(1)} %slice.283), channel_id=1, source_target_pairs={{0,1},{1,0},{2,3},{3,2},{4,5},{5,4},{6,7},{7,6},{8,9},{9,8},{10,11... | collective-permute-start | bytes 2359304 | tf_op jit(solution)/shard_map/ppermute | solution.py:33
  267.5 5.1 %collective-permute-start.27 = (f32[5952]{0:T(1024)S(1)}, f32[5952]{0:T(1024)S(1)}, u32[]{:S(2)}, u32[]{:S(2)}) collective-permute-start(f32[5952]{0:T(1024)S(1)} %add.340), channel_id=1, source_target_pairs={{0,8},{4,12},{8,0},{12,4},{16,24},{20,28},{24,16},{28,20},{1,9},{5... | collective-permute-start | bytes 71432 | tf_op jit(solution)/shard_map/ppermute | solution.py:33
  270.5 14.3 %collective-permute-start.19 = (bf16[192,768]{1,0:T(8,128)(2,1)S(1)}, bf16[192,768]{1,0:T(8,128)(2,1)S(1)}, u32[]{:S(2)}, u32[]{:S(2)}) collective-permute-start(bf16[192,768]{1,0:T(8,128)(2,1)S(1)} %dynamic-slice_convert_fusion.2), channel_id=1, source_target_pairs={{0,8},{4,12},{8,0},{12,4},{16,24},{20,28},{24,16},{28,20},{1,9},{5... | collective-permute-start | bytes 884744 | tf_op jit(solution)/shard_map/ppermute | solution.py:33
  270.7 24.0 %collective-permute-start.42 = (bf16[96,768]{1,0:T(8,128)(2,1)S(1)}, bf16[96,768]{1,0:T(8,128)(2,1)S(1)}, u32[]{:S(2)}, u32[]{:S(2)}) collective-permute-start(bf16[96,768]{1,0:T(8,128)(2,1)S(1)} %add_convert_fusion.8), channel_id=1, source_target_pairs={{0,16},{4,20},{8,24},{12,28},{16,0},{20,4},{24,8},{28,12},{1,17},{... | collective-permute-start | bytes 442376 | tf_op jit(solution)/shard_map/ppermute | solution.py:33
  272.6 9.1 %collective-permute-start.28 = (f32[5952]{0:T(1024)S(1)}, f32[5952]{0:T(1024)S(1)}, u32[]{:S(2)}, u32[]{:S(2)}) collective-permute-start(f32[5952]{0:T(1024)S(1)} %add.341), channel_id=1, source_target_pairs={{0,16},{4,20},{8,24},{12,28},{16,0},{20,4},{24,8},{28,12},{1,17},{... | collective-permute-start | bytes 71432 | tf_op jit(solution)/shard_map/ppermute | solution.py:33
  274.0 22.8 %collective-permute-start.34 = (bf16[192,384]{1,0:T(8,128)(2,1)S(1)}, bf16[192,384]{1,0:T(8,128)(2,1)S(1)}, u32[]{:S(2)}, u32[]{:S(2)}) collective-permute-start(bf16[192,384]{1,0:T(8,128)(2,1)S(1)} %add_convert_fusion.9), channel_id=1, source_target_pairs={{0,16},{4,20},{8,24},{12,28},{16,0},{20,4},{24,8},{28,12},{1,17},{... | collective-permute-start | bytes 442376 | tf_op jit(solution)/shard_map/ppermute | solution.py:33
  285.0 9.5 %collective-permute-start.20 = (bf16[96,768]{1,0:T(8,128)(2,1)S(1)}, bf16[96,768]{1,0:T(8,128)(2,1)S(1)}, u32[]{:S(2)}, u32[]{:S(2)}) collective-permute-start(bf16[96,768]{1,0:T(8,128)(2,1)S(1)} %dynamic-slice_convert_fusion.5), channel_id=1, source_target_pairs={{0,16},{4,20},{8,24},{12,28},{16,0},{20,4},{24,8},{28,12},{1,17},{... | collective-permute-start | bytes 442376 | tf_op jit(solution)/shard_map/ppermute | solution.py:33
  294.5 8.6 %collective-permute-start.21 = (bf16[96,768]{1,0:T(8,128)(2,1)S(1)}, bf16[96,768]{1,0:T(8,128)(2,1)S(1)}, u32[]{:S(2)}, u32[]{:S(2)}) collective-permute-start(bf16[96,768]{1,0:T(8,128)(2,1)S(1)} %add_convert_fusion.10), channel_id=1, source_target_pairs={{0,16},{4,20},{8,24},{12,28},{16,0},{20,4},{24,8},{28,12},{1,17},{... | collective-permute-start | bytes 442376 | tf_op jit(solution)/shard_map/ppermute | solution.py:33
  294.7 13.1 %collective-permute-start.43 = (bf16[192,768]{1,0:T(8,128)(2,1)S(1)}, bf16[192,768]{1,0:T(8,128)(2,1)S(1)}, u32[]{:S(2)}, u32[]{:S(2)}) collective-permute-start(bf16[192,768]{1,0:T(8,128)(2,1)S(1)} %maximum_select_fusion.9), channel_id=1, source_target_pairs={{0,8},{4,12},{8,0},{12,4},{16,24},{20,28},{24,16},{28,20},{1,9},{5... | collective-permute-start | bytes 884744 | tf_op jit(solution)/shard_map/ppermute | solution.py:33
  296.8 17.3 %collective-permute-start.35 = (bf16[384,384]{1,0:T(8,128)(2,1)S(1)}, bf16[384,384]{1,0:T(8,128)(2,1)S(1)}, u32[]{:S(2)}, u32[]{:S(2)}) collective-permute-start(bf16[384,384]{1,0:T(8,128)(2,1)S(1)} %maximum_select_fusion.8), channel_id=1, source_target_pairs={{0,8},{4,12},{8,0},{12,4},{16,24},{20,28},{24,16},{28,20},{1,9},{5... | collective-permute-start | bytes 884744 | tf_op jit(solution)/shard_map/ppermute | solution.py:33
  303.2 16.0 %collective-permute-start.22 = (bf16[192,768]{1,0:T(8,128)(2,1)S(1)}, bf16[192,768]{1,0:T(8,128)(2,1)S(1)}, u32[]{:S(2)}, u32[]{:S(2)}) collective-permute-start(bf16[192,768]{1,0:T(8,128)(2,1)S(1)} %maximum_select_fusion.7), channel_id=1, source_target_pairs={{0,8},{4,12},{8,0},{12,4},{16,24},{20,28},{24,16},{28,20},{1,9},{5... | collective-permute-start | bytes 884744 | tf_op jit(solution)/shard_map/ppermute | solution.py:33
  303.9 17.5 %copy-start.11 = (f32[512,768]{1,0:T(8,128)S(1)}, f32[512,768]{1,0:T(8,128)}, u32[]{:S(2)}) copy-start(f32[512,768]{1,0:T(8,128)} %get-tuple-element.54) | copy-start | bytes 4718596
  308.0 16.3 %collective-permute-start.44 = (bf16[384,768]{1,0:T(8,128)(2,1)S(1)}, bf16[384,768]{1,0:T(8,128)(2,1)S(1)}, u32[]{:S(2)}, u32[]{:S(2)}) collective-permute-start(bf16[384,768]{1,0:T(8,128)(2,1)S(1)} %maximum_select_fusion.6), channel_id=1, source_target_pairs={{0,4},{4,0},{8,12},{12,8},{16,20},{20,16},{24,28},{28,24},{1,5},{5... | collective-permute-start | bytes 1769480 | tf_op jit(solution)/shard_map/ppermute | solution.py:33
  314.3 22.6 %collective-permute-start.36 = (bf16[768,384]{1,0:T(8,128)(2,1)S(1)}, bf16[768,384]{1,0:T(8,128)(2,1)S(1)}, u32[]{:S(2)}, u32[]{:S(2)}) collective-permute-start(bf16[768,384]{1,0:T(8,128)(2,1)S(1)} %maximum_select_fusion.5), channel_id=1, source_target_pairs={{0,4},{4,0},{8,12},{12,8},{16,20},{20,16},{24,28},{28,24},{1,5},{5... | collective-permute-start | bytes 1769480 | tf_op jit(solution)/shard_map/ppermute | solution.py:33
  319.5 26.9 %collective-permute-start.23 = (bf16[384,768]{1,0:T(8,128)(2,1)S(1)}, bf16[384,768]{1,0:T(8,128)(2,1)S(1)}, u32[]{:S(2)}, u32[]{:S(2)}) collective-permute-start(bf16[384,768]{1,0:T(8,128)(2,1)S(1)} %maximum_select_fusion.4), channel_id=1, source_target_pairs={{0,4},{4,0},{8,12},{12,8},{16,20},{20,16},{24,28},{28,24},{1,5},{5... | collective-permute-start | bytes 1769480 | tf_op jit(solution)/shard_map/ppermute | solution.py:33
  (46 other events, 148.2 us)
